TPU v7x, 256 devices: a whole 4x4x8 slice. The times are simulated.
256 devices in a mesh: leaf: 16 (over z, x_lo), seq: 16 (over x_hi, y, core).
Axes of the slice: x: 4 (x_hi: 2, x_lo: 2; x = x_hi * 2 + x_lo), y: 4, z: 8, core: 2. Of those that a mesh axis runs over, the one named last changes fastest.
Arguments:
- query_raw: bfloat16 [16, 5120, 2048], P('leaf', 'seq'), may hold values from -6 to 6
- key_raw: bfloat16 [16, 5120, 512], P('leaf', 'seq'), may hold values from -6 to 6
- value_raw: bfloat16 [16, 5120, 512], P('leaf', 'seq'), may hold values from -6 to 6
- grad_out: bfloat16 [16, 5120, 2048], P('leaf', 'seq'), may hold values from -6 to 6
- query_gain: float32 [128], replicated, may hold values from 0.5 to 1.5
- key_gain: float32 [128], replicated, may hold values from 0.5 to 1.5
- leaf_parent: int32 [16, 16], P('leaf', 'seq'), may hold values from 0 to 3
- leaf_blocks: int32 [16, 16], P('leaf', 'seq'), may hold values from 1 to 3, as said below
Outputs:
- grad_query: bfloat16 [16, 5120, 2048], P('leaf', 'seq')
- grad_key: bfloat16 [16, 5120, 512], P('leaf', 'seq')
- grad_value: bfloat16 [16, 5120, 512], P('leaf', 'seq')
- query_gain_grad: float32 [128], replicated
- key_gain_grad: float32 [128], replicated
Inputs may be any that keep to these rules, and one draw needn't show every extreme that they name: `leaf_blocks`: in every tree some leaf has all 3 blocks.
All inputs are finite; a program needn't handle non-finite values.
Results may differ from a plain program's by a relative error of at most 0.011.
Values may be sent and summed in bfloat16 or wider, within the bound.
A program may use at most 128 MiB of HBM per device.

v0:
```python
import jax
import jax.numpy as jnp
from jax import lax
from jax.sharding import PartitionSpec as P

HQ = 16
HK = 4
DH = 128
R_DEV = 64
B_DEV = 64
LEAF_BLOCK = 64
GROUP = 4
L_DEV = 192


EPS = 1e-06


def contract(form, left, right):
    return jnp.einsum(form, left, right, preferred_element_type=jnp.float32)


def normalize(raw, gain):
    values = raw.astype(jnp.float32)
    inverse = lax.rsqrt(jnp.mean(values * values, axis=-1, keepdims=True) + EPS)
    return ((values * inverse * gain).astype(jnp.bfloat16), inverse)


def norm_backward(raw, inverse, gain, upstream):
    values = raw.astype(jnp.float32)
    scaled = upstream * gain
    grad_raw = inverse * scaled - values * inverse * inverse * inverse * jnp.mean(
        scaled * values, axis=-1, keepdims=True
    )
    grad_gain = jnp.sum((upstream * values * inverse).reshape(-1, values.shape[-1]), axis=0)
    return (grad_raw.astype(jnp.bfloat16), grad_gain)


def query_major(flat, kv_heads, head_dim):
    return flat.reshape(flat.shape[0], kv_heads, -1, head_dim).transpose(1, 0, 2, 3)


def key_major(flat, kv_heads, head_dim):
    return flat.reshape(flat.shape[0], kv_heads, head_dim).transpose(1, 0, 2)


def key_flat(major):
    return major.transpose(1, 0, 2).reshape(major.shape[1], -1)


def query_flat(major):
    return major.transpose(1, 0, 2, 3).reshape(major.shape[1], -1)


def forward_terms(query, keys, values, allowed):
    scale = query.shape[-1] ** (-0.5)
    scores = contract("qgd,jd->gqj", query, keys) * scale
    expos = jnp.where(allowed[None], jnp.exp(scores), 0.0)
    total = jnp.sum(expos, axis=-1)
    weighted = contract("gqj,jd->qgd", expos.astype(jnp.bfloat16), values)
    return (total, weighted)


def backward_terms(query, keys, values, upstream, allowed, total, dot_row):
    scale = query.shape[-1] ** (-0.5)
    scores = contract("qgd,jd->gqj", query, keys) * scale
    probs = jnp.where(allowed[None], jnp.exp(scores), 0.0) / total[:, :, None]
    grad_probs = contract("qgd,jd->gqj", upstream, values)
    grad_scores = (probs * (grad_probs - dot_row[:, :, None])).astype(jnp.bfloat16)
    grad_query = contract("gqj,jd->qgd", grad_scores, keys) * scale
    grad_keys = contract("gqj,qgd->jd", grad_scores, query) * scale
    grad_values = contract("gqj,qgd->jd", probs.astype(jnp.bfloat16), upstream)
    return (grad_query, grad_keys, grad_values)


def set_forward(query_h, keys_h, values_h, allowed):

    def one_head(bundle):
        return forward_terms(bundle[0], bundle[1], bundle[2], allowed)

    return lax.map(one_head, (query_h, keys_h, values_h))


def set_backward(query_h, keys_h, values_h, upstream_h, allowed, total_h, dot_h):

    def one_head(bundle):
        return backward_terms(
            bundle[0], bundle[1], bundle[2], bundle[3], allowed, bundle[4], bundle[5]
        )

    return lax.map(one_head, (query_h, keys_h, values_h, upstream_h, total_h, dot_h))


def root_forward(query_h, piece_keys, piece_values, limit, kv_heads, head_dim):
    span = piece_keys.shape[0]
    allowed = jnp.arange(span, dtype=jnp.int32)[None, :] < limit[:, None]
    return set_forward(
        query_h,
        key_major(piece_keys, kv_heads, head_dim),
        key_major(piece_values, kv_heads, head_dim),
        allowed,
    )


def root_backward(
    query_h, upstream_h, piece_keys, piece_values, limit, total, dot_h, kv_heads, head_dim
):
    span = piece_keys.shape[0]
    allowed = jnp.arange(span, dtype=jnp.int32)[None, :] < limit[:, None]
    grad_query, grad_keys, grad_values = set_backward(
        query_h,
        key_major(piece_keys, kv_heads, head_dim),
        key_major(piece_values, kv_heads, head_dim),
        upstream_h,
        allowed,
        total,
        dot_h,
    )
    return (grad_query, key_flat(grad_keys), key_flat(grad_values))


def side_sets(
    device_index,
    parent,
    leaf_length,
    keys_loc,
    values_loc,
    branch_keys,
    branch_values,
    kv_heads,
    head_dim,
):
    span = GROUP * B_DEV
    own_start = device_index // GROUP * span
    parent_start = parent * span
    own_query = device_index % GROUP * B_DEV + jnp.arange(B_DEV, dtype=jnp.int32)
    key_ids = jnp.arange(span, dtype=jnp.int32)
    own_allowed = key_ids[None, :] <= own_query[:, None]
    leaf_ids = jnp.arange(L_DEV, dtype=jnp.int32)
    leaf_allowed = (leaf_ids[None, :] <= leaf_ids[:, None]) & (leaf_ids[None, :] < leaf_length)
    parent_allowed = jnp.zeros((L_DEV, span), jnp.int32) == 0

    def heads(flat):
        return key_major(flat, kv_heads, head_dim)

    own_set = (
        R_DEV,
        B_DEV,
        heads(lax.dynamic_slice_in_dim(branch_keys, own_start, span, 0)),
        heads(lax.dynamic_slice_in_dim(branch_values, own_start, span, 0)),
        own_allowed,
    )
    parent_set = (
        R_DEV + B_DEV,
        L_DEV,
        heads(lax.dynamic_slice_in_dim(branch_keys, parent_start, span, 0)),
        heads(lax.dynamic_slice_in_dim(branch_values, parent_start, span, 0)),
        parent_allowed,
    )
    leaf_set = (
        R_DEV + B_DEV,
        L_DEV,
        heads(keys_loc[R_DEV + B_DEV :]),
        heads(values_loc[R_DEV + B_DEV :]),
        leaf_allowed,
    )
    return ([own_set, parent_set, leaf_set], own_start, parent_start)


def add_sides_forward(query_h, total, weighted, sets):
    for row_start, count, keys_h, values_h, allowed in sets:
        row_stop = row_start + count
        part_total, part_weighted = set_forward(
            query_h[:, row_start:row_stop], keys_h, values_h, allowed
        )
        total = total.at[:, :, row_start:row_stop].add(part_total)
        weighted = weighted.at[:, row_start:row_stop].add(part_weighted)
    return (total, weighted)


def dot_rows(upstream_h, weighted, total):
    output = weighted / jnp.transpose(total, (0, 2, 1))[..., None]
    return jnp.transpose(jnp.sum(upstream_h.astype(jnp.float32) * output, axis=-1), (0, 2, 1))


def add_sides_backward(query_h, upstream_h, total, dot_h, grad_q, sets):
    key_grads = []
    for row_start, count, keys_h, values_h, allowed in sets:
        row_stop = row_start + count
        part_q, part_k, part_v = set_backward(
            query_h[:, row_start:row_stop],
            keys_h,
            values_h,
            upstream_h[:, row_start:row_stop],
            allowed,
            total[:, :, row_start:row_stop],
            dot_h[:, :, row_start:row_stop],
        )
        grad_q = grad_q.at[:, row_start:row_stop].add(part_q)
        key_grads.append((key_flat(part_k), key_flat(part_v)))
    return (grad_q, key_grads)


def branch_partials(key_grads, own_start, parent_start, total_rows, width):
    grad_k = jnp.zeros((total_rows, width), jnp.float32)
    grad_v = jnp.zeros((total_rows, width), jnp.float32)
    for grads, offset in zip(key_grads[:2], (own_start, parent_start)):
        span = grads[0].shape[0]
        grad_k = lax.dynamic_update_slice_in_dim(
            grad_k, lax.dynamic_slice_in_dim(grad_k, offset, span, 0) + grads[0], offset, 0
        )
        grad_v = lax.dynamic_update_slice_in_dim(
            grad_v, lax.dynamic_slice_in_dim(grad_v, offset, span, 0) + grads[1], offset, 0
        )
    return (grad_k, grad_v)


def on_device(
    query_raw, key_raw, value_raw, grad_out, query_gain, key_gain, leaf_parent, leaf_blocks
):
    seq_count = lax.axis_size("seq")
    device_index = lax.axis_index("seq")
    row_count = query_raw.shape[1]
    width_kv = key_raw.shape[2]
    shaped_q = query_raw[0].reshape(row_count, HQ, DH)
    shaped_k = key_raw[0].reshape(row_count, HK, DH)
    query_n, query_inverse = normalize(shaped_q, query_gain)
    keys_n, keys_inverse = normalize(shaped_k, key_gain)
    query_n = query_n.reshape(row_count, -1)
    keys_n = keys_n.reshape(row_count, -1)
    values_loc = value_raw[0]
    parent = leaf_parent[0, 0]
    blocks = leaf_blocks[0, 0]
    branch_keys, branch_values = (
        lax.all_gather(keys_n[R_DEV : R_DEV + B_DEV], "seq", axis=0, tiled=True),
        lax.all_gather(values_loc[R_DEV : R_DEV + B_DEV], "seq", axis=0, tiled=True),
    )
    root_total = R_DEV * seq_count
    row_ids = jnp.arange(row_count, dtype=jnp.int32)
    limit = jnp.where(row_ids < R_DEV, device_index * R_DEV + row_ids + 1, root_total)
    leaf_length = blocks * LEAF_BLOCK
    valid = (row_ids < R_DEV + B_DEV) | (row_ids - R_DEV - B_DEV < leaf_length)
    upstream = jnp.where(valid[:, None], grad_out[0], jnp.zeros_like(grad_out[0]))
    query_h = query_major(query_n, HK, DH)
    upstream_h = query_major(upstream, HK, DH)
    sets, own_start, parent_start = side_sets(
        device_index, parent, leaf_length, keys_n, values_loc, branch_keys, branch_values, HK, DH
    )
    root_pieces = (keys_n[:R_DEV], values_loc[:R_DEV])
    root_keys, root_values = (
        lax.all_gather(root_pieces[0], "seq", axis=0, tiled=True),
        lax.all_gather(root_pieces[1], "seq", axis=0, tiled=True),
    )
    pieces = (root_keys, root_values)
    part_total, part_weighted = root_forward(query_h, pieces[0], pieces[1], limit, HK, DH)
    total, weighted = add_sides_forward(query_h, part_total, part_weighted, sets)
    dot_h = dot_rows(upstream_h, weighted, total)
    pieces = (root_keys, root_values)
    part_q, part_k, part_v = root_backward(
        query_h, upstream_h, pieces[0], pieces[1], limit, total, dot_h, HK, DH
    )
    grad_q, key_grads = add_sides_backward(query_h, upstream_h, total, dot_h, part_q, sets)
    branch_gk, branch_gv = branch_partials(
        key_grads, own_start, parent_start, branch_keys.shape[0], width_kv
    )
    grad_query, query_gain_part = norm_backward(
        shaped_q, query_inverse, query_gain, query_flat(grad_q).reshape(row_count, HQ, DH)
    )
    root_share_k, root_share_v, branch_share_k, branch_share_v = (
        lax.psum_scatter(part_k, "seq", scatter_dimension=0, tiled=True),
        lax.psum_scatter(part_v, "seq", scatter_dimension=0, tiled=True),
        lax.psum_scatter(branch_gk, "seq", scatter_dimension=0, tiled=True),
        lax.psum_scatter(branch_gv, "seq", scatter_dimension=0, tiled=True),
    )
    grad_keys_all = jnp.concatenate([root_share_k, branch_share_k, key_grads[2][0]], axis=0)
    grad_value = jnp.concatenate([root_share_v, branch_share_v, key_grads[2][1]], axis=0).astype(
        jnp.bfloat16
    )
    grad_key, key_gain_part = norm_backward(
        shaped_k, keys_inverse, key_gain, grad_keys_all.reshape(row_count, HK, DH)
    )
    query_gain_sum, key_gain_sum = lax.psum((query_gain_part, key_gain_part), ("leaf", "seq"))
    return (
        grad_query.reshape(1, row_count, -1),
        grad_key.reshape(1, row_count, -1),
        grad_value.reshape(1, row_count, -1),
        query_gain_sum,
        key_gain_sum,
    )


def solution(mesh):
    return jax.shard_map(
        on_device,
        mesh=mesh,
        in_specs=(
            P("leaf", "seq", None),
            P("leaf", "seq", None),
            P("leaf", "seq", None),
            P("leaf", "seq", None),
            P(),
            P(),
            P("leaf", "seq"),
            P("leaf", "seq"),
        ),
        out_specs=(
            P("leaf", "seq", None),
            P("leaf", "seq", None),
            P("leaf", "seq", None),
            P(),
            P(),
        ),
        check_vma=False,
    )
```

profile of v0, /device:TPU:8, one launch (start us, length us, event | category | flops | bytes accessed | tf_op | source)
XLA Modules:
  0.0 648.0 jit_solution(6080117310424791630)
XLA Ops:
  13.4 3.2 reshape.712
  16.7 4.2 multiply_bitcast_fusion
  21.5 3.9 copy.417
  32.2 4.8 while.123
  37.1 4.5 squeeze.107
  41.6 22.2 %all-gather.7.cloned.1.call-done = bf16[1024,512]{1,0:T(8,128)(2,1)} async-done(((bf16[64,512]{1,0:T(8,128)(2,1)}), bf16[1024,512]{1,0:T(8,128)(2,1)}) %all-gather.7.cloned.1.call-update) | async-done | bytes 1048592 | tf_op jit(solution)/shard_map/all_gather | solution.py:251
  67.7 47.5 %all-gather.11.cloned.1.call-done = bf16[1,1024,512]{2,1,0:T(8,128)(2,1)} async-done(((bf16[1,64,512]{2,1,0:T(8,128)(2,1)}), bf16[1,1024,512]{2,1,0:T(8,128)(2,1)}) %all-gather.11.cloned.1.call-update) | async-done | bytes 1048592 | tf_op jit(solution)/shard_map/all_gather | solution.py:252
  119.1 20.7 %while.121 = (s32[]{:T(128)}, f32[4,4,320]{2,1,0:T(4,128)S(1)}, f32[4,320,4,128]{3,2,0,1:T(4,128)}, bf16[4,1024,128]{2,1,0:T(8,128)(2,1)S(1)}, bf16[4,320,4,128]...) while((s32[]{:T(128)}, f32[4,4,320]{2,1,0:T(4,128)S(1)}, ...), condition=%wide.region_4.5_spmd.clone, body=%wide.region_2.4_spmd.clone.sunk | while | flops 679279360 | bytes 14306665 | solution.py:81
  139.8 26.9 %all-gather.9.cloned.1.call-done = bf16[1024,512]{1,0:T(8,128)(2,1)} async-done(((bf16[64,512]{1,0:T(8,128)(2,1)}), bf16[1024,512]{1,0:T(8,128)(2,1)}) %all-gather.9.cloned.1.call-update) | async-done | bytes 1048592 | tf_op jit(solution)/shard_map/all_gather | solution.py:235
  169.4 48.5 %all-gather.13.cloned.1.call-done = bf16[1,1024,512]{2,1,0:T(8,128)(2,1)} async-done(((bf16[1,64,512]{2,1,0:T(8,128)(2,1)}), bf16[1,1024,512]{2,1,0:T(8,128)(2,1)}) %all-gather.13.cloned.1.call-update) | async-done | bytes 1048592 | tf_op jit(solution)/shard_map/all_gather | solution.py:236
  221.7 8.9 %while.122 = (s32[]{:T(128)}, f32[4,4,64]{2,1,0:T(4,128)S(1)}, f32[4,64,4,128]{3,2,0,1:T(4,128)}, bf16[4,256,128]{2,1,0:T(8,128)(2,1)}, bf16[4,64,4,128]{3,1,2,0...) while((s32[]{:T(128)}, f32[4,4,64]{2,1,0:T(4,128)S(1)}, ...), condition=%wide.region_7.8_spmd.clone, body=%wide.region_5.7_spmd.clone.sunk | while | flops 33832704 | bytes 891241 | solution.py:81
  230.7 11.1 %scatter-add.30 = f32[4,4,320]{2,1,0:T(4,128)S(1)} dynamic-update-slice(f32[4,4,320]{2,1,0:T(4,128)S(1)} %get-tuple-element.491, f32[4,4,64]{2,1,0:T(4,128)S(1)} %slice_add_fusion.3, s32[]{:T(128)} %copy.583, s32[]{:T(128)} %copy.583, s32[]{:T(128)} %constant.424.clone.1) | dynamic-update-slice | bytes 8196 | tf_op jit(solution)/shard_map/scatter-add | solution.py:176
  244.5 4.3 while.119
  260.1 5.5 fusion.198
  272.9 19.3 %while.125 = (s32[]{:T(128)}, f32[4,64,4,128]{3,1,2,0:T(8,128)}, f32[4,256,128]{2,1,0:T(8,128)}, f32[4,256,128]{2,1,0:T(8,128)}, bf16[4,256,128]{2,1,0:T(8,128)(...) while((s32[]{:T(128)}, f32[4,64,4,128]{3,1,2,0:T(8,128)}, ...), condition=%wide.region_18.19_spmd.clone, body=%wide.region_17.18_spmd.clone.sunk | while | flops 84426752 | bytes 2206093 | solution.py:91
  294.5 14.6 %while.120 = (s32[]{:T(128)}, f32[4,192,4,128]{3,1,2,0:T(8,128)S(1)}, f32[4,256,128]{2,1,0:T(8,128)}, f32[4,256,128]{2,1,0:T(8,128)}, bf16[4,256,128]{2,1,0:T(8,...) while((s32[]{:T(128)}, ...), condition=%wide.region_20.21_spmd, body=%wide.region_19.20_spmd.sunk | while | flops 252968960 | bytes 5203065 | solution.py:91
  314.7 51.0 %while.124 = (s32[]{:T(128)}, f32[4,320,4,128]{3,1,2,0:T(8,128)}, f32[4,1024,128]{2,1,0:T(8,128)}, f32[4,1024,128]{2,1,0:T(8,128)}, bf16[4,1024,128]{2,1,0:T(8,1...) while((s32[]{:T(128)}, f32[4,320,4,128]{3,1,2,0:T(8,128)}, ...), condition=%wide.region_16.17_spmd.clone, body=%wide.region_15.16_spmd.clone.sunk | while | flops 1687519232 | bytes 28739980 | solution.py:91
  323.1 2.7 fusion.347
  335.9 2.7 fusion.347
  358.7 2.7 fusion.346
  361.4 2.7 fusion.347
  365.8 3.3 copy_bitcast_fusion.7
  381.3 31.5 %while.126 = (s32[]{:T(128)}, f32[4,192,4,128]{3,1,2,0:T(8,128)S(1)}, f32[4,192,128]{2,1,0:T(8,128)}, bf16[4,192,128]{2,1,0:T(8,128)(2,1)}, bf16[4,192,128]{2,1,...) while((s32[]{:T(128)}, ...), condition=%wide.region_22.23_spmd.clone, body=%wide.region_21.22_spmd.clone.sunk | while | flops 189972480 | bytes 6340985 | solution.py:91
  422.0 2.7 add_dynamic-update-slice_fusion
  429.3 3.7 mul.369
  433.0 3.2 copy.367
  436.3 4.3 reshape_reshape.4
  441.9 5.6 fusion.197
  448.5 26.1 %reduce-scatter.5.cloned.1.call-done = f32[64,512]{1,0:T(8,128)} async-done(((f32[1024,512]{1,0:T(8,128)}), f32[64,512]{1,0:T(8,128)}) %reduce-scatter.5.cloned.1.call-update) | async-done | bytes 131088 | tf_op jit(solution)/shard_map/reduce_scatter | solution.py:270
  478.8 74.2 %all-reduce = (f32[128]{0:T(128)}, f32[128]{0:T(128)}) all-reduce(f32[128]{0:T(128)S(1)} %get-tuple-element.1057, f32[128]{0:T(128)S(1)} %bitcast_reduce_fusion), channel_id=1, replica_groups=mesh['leaf'=16,'seq'=16] {'leaf','seq'}, use_global_device_ids=true, to_apply=%region_30.31 | all-reduce | flops 256 | bytes 2048 | tf_op jit(solution)/shard_map/psum | solution.py:282
  553.0 3.6 reduce-scatter.11.cloned.1.call-done
  557.5 81.6 %reduce-scatter.9.cloned.1.call-done = f32[64,512]{1,0:T(8,128)} async-done(((f32[1024,512]{1,0:T(8,128)}), f32[64,512]{1,0:T(8,128)}) %reduce-scatter.9.cloned.1.call-update) | async-done | bytes 131088 | tf_op jit(solution)/shard_map/reduce_scatter | solution.py:271
  (431 shorter events, 233.4 us)
Async XLA Ops:
  7.2 56.6 %all-gather.7.cloned.1.call-start = ((), (), s32[]{:S(2)}) async-start(), calls=%async_computation.4 | async-start | bytes 1114112 | tf_op jit(solution)/shard_map/all_gather | solution.py:251
  11.3 103.9 %all-gather.11.cloned.1.call-start = ((), (), s32[]{:S(2)}) async-start(), calls=%async_computation.10 | async-start | bytes 1114112 | tf_op jit(solution)/shard_map/all_gather | solution.py:252
  12.1 154.6 %all-gather.9.cloned.1.call-start = ((), (), s32[]{:S(2)}) async-start(), calls=%async_computation.5 | async-start | bytes 1114112 | tf_op jit(solution)/shard_map/all_gather | solution.py:235
  12.8 205.2 %all-gather.13.cloned.1.call-start = ((), (), s32[]{:S(2)}) async-start(), calls=%async_computation.11 | async-start | bytes 1114112 | tf_op jit(solution)/shard_map/all_gather | solution.py:236
  13.4 434.1 %reduce-scatter.7.cloned.1.call-start = ((), (), s32[]{:S(2)}) async-start(), calls=%async_computation.7 | async-start | bytes 2228224 | tf_op jit(solution)/shard_map/reduce_scatter | solution.py:272
  16.7 11.4 %copy-start = (f32[320,4,4,128]{3,2,1,0:T(4,128)}, f32[320,4,4,128]{3,2,1,0:T(4,128)S(1)}, u32[]{:S(2)}) copy-start(f32[320,4,4,128]{3,2,1,0:T(4,128)S(1)} %reshape.712) | copy-start | bytes 7864324
  37.0 29.1 %copy-start.21 = (bf16[4,192,128]{2,1,0:T(8,128)(2,1)}, bf16[4,192,128]{2,1,0:T(8,128)(2,1)S(1)}, u32[]{:S(2)}) copy-start(bf16[4,192,128]{2,1,0:T(8,128)(2,1)S(1)} %get-tuple-element.1954) | copy-start | bytes 589828
  37.0 29.1 %copy-start.32 = (bf16[4,192,128]{2,1,0:T(8,128)(2,1)}, bf16[4,192,128]{2,1,0:T(8,128)(2,1)S(1)}, u32[]{:S(2)}) copy-start(bf16[4,192,128]{2,1,0:T(8,128)(2,1)S(1)} %get-tuple-element.1960) | copy-start | bytes 589828
  37.0 30.7 %copy-start.12 = (f32[4,192,4,128]{3,2,0,1:T(4,128)}, f32[4,192,4,128]{3,2,0,1:T(4,128)S(1)}, u32[]{:S(2)}) copy-start(f32[4,192,4,128]{3,2,0,1:T(4,128)S(1)} %get-tuple-element.498) | copy-start | bytes 4718596
  37.1 30.7 %copy-start.43 = (pred[192]{0:T(512)(128)(4,1)}, pred[192]{0:T(512)(128)(4,1)S(1)}, u32[]{:S(2)}) copy-start(pred[192]{0:T(512)(128)(4,1)S(1)} %get-tuple-element.1978) | copy-start | bytes 580
  139.8 81.9 %copy-start.13 = (bf16[4,1024,128]{2,1,0:T(8,128)(2,1)}, bf16[4,1024,128]{2,1,0:T(8,128)(2,1)S(1)}, u32[]{:S(2)}) copy-start(bf16[4,1024,128]{2,1,0:T(8,128)(2,1)S(1)} %get-tuple-element.1949) | copy-start | bytes 3145732
  139.8 81.9 %copy-start.14 = (bf16[4,1024,128]{2,1,0:T(8,128)(2,1)}, bf16[4,1024,128]{2,1,0:T(8,128)(2,1)S(1)}, u32[]{:S(2)}) copy-start(bf16[4,1024,128]{2,1,0:T(8,128)(2,1)S(1)} %get-tuple-element.1950) | copy-start | bytes 3145732
  230.6 13.7 %copy-start.19 = (bf16[4,256,128]{2,1,0:T(8,128)(2,1)}, bf16[4,256,128]{2,1,0:T(8,128)(2,1)S(1)}, u32[]{:S(2)}) copy-start(bf16[4,256,128]{2,1,0:T(8,128)(2,1)S(1)} %get-tuple-element.1953) | copy-start | bytes 786436
  244.5 5.6 copy-start.35
  265.6 5.5 copy-start.16
  265.6 7.3 %copy-start.27 = (bf16[4,64,4,128]{3,1,2,0:T(8,128)(2,1)S(1)}, bf16[4,64,4,128]{3,1,2,0:T(8,128)(2,1)}, u32[]{:S(2)}) copy-start(bf16[4,64,4,128]{3,1,2,0:T(8,128)(2,1)} %get-tuple-element.1955) | copy-start | bytes 786436
  265.6 7.3 %copy-start.28 = (bf16[4,256,128]{2,1,0:T(8,128)(2,1)S(1)}, bf16[4,256,128]{2,1,0:T(8,128)(2,1)}, u32[]{:S(2)}) copy-start(bf16[4,256,128]{2,1,0:T(8,128)(2,1)} %get-tuple-element.1956) | copy-start | bytes 786436
  309.1 5.6 copy-start.2
  309.1 5.6 copy-start.9
  309.1 5.6 copy-start.39
  314.7 160.0 %reduce-scatter.5.cloned.1.call-start = ((), (), s32[]{:S(2)}) async-start(), calls=%async_computation.6 | async-start | bytes 2228224 | tf_op jit(solution)/shard_map/reduce_scatter | solution.py:270
  369.1 187.5 %reduce-scatter.11.cloned.1.call-start = ((), (), s32[]{:S(2)}) async-start(), calls=%async_computation.9 | async-start | bytes 2228224 | tf_op jit(solution)/shard_map/reduce_scatter | solution.py:273
  381.1 258.0 %reduce-scatter.9.cloned.1.call-start = ((), (), s32[]{:S(2)}) async-start(), calls=%async_computation.8 | async-start | bytes 2228224 | tf_op jit(solution)/shard_map/reduce_scatter | solution.py:271
  382.9 5.5 copy-start.40
  436.3 5.6 copy-start.5
  436.3 5.6 copy-start.44
  441.9 33.6 %copy-start.8 = (f32[320,4,128]{2,1,0:T(4,128)S(1)}, f32[320,4,128]{2,1,0:T(4,128)}, u32[]{:S(2)}) copy-start(f32[320,4,128]{2,1,0:T(4,128)} %copy-done.7) | copy-start | bytes 1966084
  441.9 33.6 %copy-start.26 = (f32[4,192,128]{2,1,0:T(8,128)S(1)}, f32[4,192,128]{2,1,0:T(8,128)}, u32[]{:S(2)}) copy-start(f32[4,192,128]{2,1,0:T(8,128)} %get-tuple-element.506) | copy-start | bytes 1179652
  441.9 33.7 %copy-start.46 = (f32[128]{0:T(128)S(1)}, f32[128]{0:T(128)}, u32[]{:S(2)}) copy-start(f32[128]{0:T(128)} %param.47) | copy-start | bytes 1540
  447.5 29.2 %copy-start.45 = (f32[512]{0:T(512)S(1)}, f32[512]{0:T(512)}, u32[]{:S(2)}) copy-start(f32[512]{0:T(512)} %broadcast_bitcast_fusion.1) | copy-start | bytes 6148
  447.5 29.2 %copy-start.36 = (f32[64,512]{1,0:T(8,128)S(1)}, f32[64,512]{1,0:T(8,128)}, u32[]{:S(2)}) copy-start(f32[64,512]{1,0:T(8,128)} %reduce-scatter.7.cloned.1.call-done) | copy-start | bytes 393220
  476.0 164.0 %copy-start.34 = (bf16[1,192,512]{2,1,0:T(8,128)(2,1)S(1)}, bf16[1,192,512]{2,1,0:T(8,128)(2,1)}, u32[]{:S(2)}) copy-start(bf16[1,192,512]{2,1,0:T(8,128)(2,1)} %concatenate.72) | copy-start | bytes 589828
  (32 other events, 82.9 us)
Sparse Core Ops, SparseCore 0:
  11.4 52.3 all-gather.6
  66.6 48.6 all-gather.10
  118.0 48.6 all-gather.8
  169.3 48.6 all-gather.12
  314.8 77.4 reduce-scatter.6
  396.9 77.7 reduce-scatter.4
  478.8 77.7 reduce-scatter.10
  561.4 77.6 reduce-scatter.8
where the time goes:
time: 661 us; the launch traced here: 648 us
  waiting for transfers between devices  257 us (39%)
  local copies, waits for them, and re-layouts  127 us (19%)
  matrix products  124 us (19%)
  blocking collectives  74.2 us (11%)
  other arithmetic  47.9 us (7%)
  between operations  16.7 us (3%)
    dot_general x112, matrix products, contract(): return jnp.einsum(form, left, right, preferred_element_type=jnp.float32)  124 us
    reduce_scatter x1, waiting for transfers between devices, on_device(): lax.psum_scatter(part_v, 'seq', scatter_dimension=0, tiled=True)  81.6 us
    psum x1, blocking collectives, on_device(): lax.psum((query_gain_part, key_gain_part), ('leaf', 'seq'))  74.2 us
    all_gather x1, waiting for transfers between devices, on_device(): lax.all_gather(values_loc[R_DEV:R_DEV + B_DEV], 'seq', axis=0, tiled=True)  48.5 us
    all_gather x1, waiting for transfers between devices, on_device(): lax.all_gather(root_pieces[1], 'seq', axis=0, tiled=True)  47.5 us
    all_gather x1, waiting for transfers between devices, on_device(): lax.all_gather(keys_n[R_DEV:R_DEV + B_DEV], 'seq', axis=0, tiled=True)  26.9 us
    reduce_scatter x1, waiting for transfers between devices, on_device(): lax.psum_scatter(part_k, 'seq', scatter_dimension=0, tiled=True)  26.1 us
    unnamed x109, local copies, waits for them, and re-layouts  23.6 us
  transfers between devices with their start and end apart: 8, of which 7 were waited for; matrix products, arithmetic and copies ran while one was open for 29% of the time, Pallas kernels for 0%

commit v1 on v0

v1 whole, which is shorter than its diff:
```python
import functools
import math

import jax
import jax.numpy as jnp
from jax import lax
from jax.experimental import pallas as pl
from jax.experimental.pallas import tpu as pltpu
from jax.sharding import PartitionSpec as P

HQ = 16
HK = 4
DH = 128
GQ = HQ // HK
R_DEV = 64
B_DEV = 64
LEAF_BLOCK = 64
L_DEV = 192
ROWS = 320
N_SEQ = 16
N_ROOT = R_DEV * N_SEQ
SPAN = 256
RB = 256
Q_ROWS = ROWS * GQ
LEAF_AT = GQ * (R_DEV + B_DEV)
EPS = 1e-06
SCALE = 1.0 / math.sqrt(DH)
EXP2_SCALE = SCALE / math.log(2.0)

F32 = jnp.float32
BF16 = jnp.bfloat16
MESH = pl.DeviceIdType.MESH
NT = (((1,), (1,)), ((), ()))
NN = (((1,), (0,)), ((), ()))
TN = (((0,), (0,)), ((), ()))

SEGMENTS = ((0, R_DEV, 0), (R_DEV, B_DEV, GQ * R_DEV), (R_DEV + B_DEV, L_DEV, LEAF_AT))

G_X, G_UP_OWN, G_DN_OWN, G_UP_PAIR, G_DN_PAIR, G_UP_FAR, G_DN_FAR, G_CORE = range(8)
N_G = G_CORE + 8
R_CORE, R_UP_FAR, R_DN_FAR, R_UP, R_DN, R_X = range(6)
N_R = 6


def dot(left, right, dims):
    return lax.dot_general(left, right, dims, preferred_element_type=F32)


def inverse_norm(values):
    return lax.rsqrt(jnp.mean(values * values, axis=-1, keepdims=True) + EPS)


def norm_backward(values, inverse, gain, upstream):
    scaled = upstream * gain
    mean = jnp.mean(scaled * values, axis=-1, keepdims=True)
    return inverse * scaled - values * (inverse * inverse * inverse * mean)


def fold(array):
    return jnp.sum(array.reshape(array.shape[0] // 8, 8, array.shape[1]), axis=0)


def kernel(
    n_leaf,
    parent_ref,
    blocks_ref,
    q_ref,
    k_ref,
    v_ref,
    u_ref,
    qgain_ref,
    kgain_ref,
    gq_ref,
    gk_ref,
    gv_ref,
    gains_ref,
    kv,
    leaf_kv,
    side,
    qn,
    up,
    expo,
    gprobs,
    gscores,
    q_scaled,
    up_scaled,
    inv_rows,
    dot_rows,
    grad_qn,
    parts,
    from_core,
    from_far,
    from_near,
    to_x,
    kept,
    from_x,
    gain_part,
    gain_seq,
    gain_leaf,
    g_send,
    g_recv,
    r_send,
    r_recv,
    a_send,
    a_recv,
    b_send,
    b_recv,
):
    me = lax.axis_index("seq")
    me_leaf = lax.axis_index("leaf")
    x = me // 8
    y = (me // 2) % 4
    c = me % 2
    y_up, y_dn, y_far = (y + 1) % 4, (y + 3) % 4, (y + 2) % 4

    def place(px, py, pc):
        return px * 8 + py * 2 + pc

    dev_core = place(x, y, 1 - c)
    dev_x = place(1 - x, y, c)
    dev_up = place(x, y_up, c)
    dev_dn = place(x, y_dn, c)
    parent = parent_ref[0, 0]
    leaf_length = blocks_ref[0, 0] * LEAF_BLOCK
    own_branch = me // 4

    barrier = pltpu.get_barrier_semaphore()

    def greet_seq(step, carry):
        pl.semaphore_signal(
            barrier, inc=1, device_id=(me_leaf, (me + step) % N_SEQ), device_id_type=MESH
        )
        return carry

    def greet_leaf(step, carry):
        pl.semaphore_signal(
            barrier, inc=1, device_id=((me_leaf + step) % n_leaf, me), device_id_type=MESH
        )
        return carry

    lax.fori_loop(1, N_SEQ, greet_seq, 0)
    lax.fori_loop(1, n_leaf, greet_leaf, 0)

    kgain = kgain_ref[...]
    own_rows = pl.ds(pl.multiple_of(me * R_DEV, R_DEV), R_DEV)
    for h in range(HK):
        cols = slice(h * DH, (h + 1) * DH)
        raw = k_ref[:, cols].astype(F32)
        normed = (raw * inverse_norm(raw) * kgain).astype(BF16)
        values = v_ref[:, cols]
        kv[h, 0, 0, own_rows, :] = normed[:R_DEV]
        kv[h, 1, 0, own_rows, :] = normed[R_DEV : R_DEV + B_DEV]
        leaf_kv[h, 0] = normed[R_DEV + B_DEV :]
        kv[h, 0, 1, own_rows, :] = values[:R_DEV]
        kv[h, 1, 1, own_rows, :] = values[R_DEV : R_DEV + B_DEV]
        leaf_kv[h, 1] = values[R_DEV + B_DEV :]

    pl.semaphore_wait(barrier, N_SEQ - 1 + n_leaf - 1)

    def piece(h, owner):
        return kv.at[h, :, :, pl.ds(pl.multiple_of(owner * R_DEV, R_DEV), R_DEV), :]

    def g_copy(h, which, owner, target):
        return pltpu.make_async_remote_copy(
            src_ref=piece(h, owner),
            dst_ref=piece(h, owner),
            send_sem=g_send.at[h, which],
            recv_sem=g_recv.at[h, which],
            device_id=(me_leaf, target),
            device_id_type=MESH,
        )

    own, pair = me, dev_x
    ring = (
        own,
        pair,
        place(x, y_dn, c),
        place(x, y_up, c),
        place(1 - x, y_dn, c),
        place(1 - x, y_up, c),
        place(0, y_far, c),
        place(1, y_far, c),
    )
    core_ring = tuple(owner + 1 - 2 * c for owner in ring)

    def gather_a(h):
        g_copy(h, G_X, own, dev_x).start()
        g_copy(h, G_UP_OWN, own, dev_up).start()
        g_copy(h, G_DN_OWN, own, dev_dn).start()
        g_copy(h, G_CORE, own, dev_core).start()

    def gather_b(h):
        g_copy(h, G_X, pair, dev_x).wait_recv()
        g_copy(h, G_UP_PAIR, pair, dev_up).start()
        g_copy(h, G_DN_PAIR, pair, dev_dn).start()
        g_copy(h, G_CORE + 1, pair, dev_core).start()

    def gather_c(h):
        g_copy(h, G_UP_OWN, ring[2], dev_dn).wait_recv()
        g_copy(h, G_DN_OWN, ring[3], dev_up).wait_recv()
        g_copy(h, G_UP_PAIR, ring[4], dev_dn).wait_recv()
        g_copy(h, G_DN_PAIR, ring[5], dev_up).wait_recv()
        g_copy(h, G_UP_FAR, place(0, y_dn, c), dev_up).start()
        g_copy(h, G_DN_FAR, place(1, y_up, c), dev_dn).start()
        for n in range(2, 6):
            g_copy(h, G_CORE + n, ring[n], dev_core).start()

    def gather_d(h):
        g_copy(h, G_UP_FAR, ring[6], dev_dn).wait_recv()
        g_copy(h, G_DN_FAR, ring[7], dev_up).wait_recv()
        for n in range(6, 8):
            g_copy(h, G_CORE + n, ring[n], dev_core).start()

    def gather_e(h):
        for n in range(8):
            g_copy(h, G_CORE + n, core_ring[n], dev_core).wait_recv()

    def gather_sent(h):
        for n in range(N_G):
            g_copy(h, n, own, dev_core).wait_send()

    def r_copy(h, which, src, dst, target):
        return pltpu.make_async_remote_copy(
            src_ref=src,
            dst_ref=dst,
            send_sem=r_send.at[h, which],
            recv_sem=r_recv.at[h, which],
            device_id=(me_leaf, target),
            device_id_type=MESH,
        )

    def r_core(h):
        return r_copy(h, R_CORE, parts.at[h, 1 - c], from_core.at[h], dev_core)

    def r_far(h):
        return (
            r_copy(h, R_UP_FAR, parts.at[h, c, y_far, 0], from_far.at[h, 0], dev_up),
            r_copy(h, R_DN_FAR, parts.at[h, c, y_far, 1], from_far.at[h, 1], dev_dn),
        )

    def r_near(h):
        return (
            r_copy(h, R_UP, parts.at[h, c, y_up], from_near.at[h, 0], dev_up),
            r_copy(h, R_DN, parts.at[h, c, y_dn], from_near.at[h, 1], dev_dn),
        )

    def r_x(h):
        return r_copy(h, R_X, to_x.at[h], from_x.at[h], dev_x)

    def added(left, right):
        return left.astype(F32) + right.astype(F32)

    def reduce_a(h):
        r_core(h).wait_recv()
        for block in range(4):
            for side_x in range(2):
                parts[h, c, block, side_x] = added(
                    parts[h, c, block, side_x], from_core[h, block, side_x]
                ).astype(BF16)
        for copy in r_far(h):
            copy.start()

    def reduce_b(h):
        for copy in r_far(h):
            copy.wait_recv()
        parts[h, c, y_up, 0] = added(parts[h, c, y_up, 0], from_far[h, 0]).astype(BF16)
        parts[h, c, y_dn, 1] = added(parts[h, c, y_dn, 1], from_far[h, 1]).astype(BF16)
        for copy in r_near(h):
            copy.start()

    def reduce_c(h):
        for copy in r_near(h):
            copy.wait_recv()

        def total(side_x):
            return added(parts[h, c, y, side_x], from_near[h, 0, side_x]) + from_near[
                h, 1, side_x
            ].astype(F32)

        to_x[h] = total(1 - x).astype(BF16)
        r_x(h).start()
        kept[h] = total(x)

    def reduce_d(h):
        r_x(h).wait_recv()
        cols = pl.ds(pl.multiple_of(h * DH, DH), DH)
        for kind, start in ((0, 0), (1, R_DEV)):
            rows = slice(start, start + R_DEV)
            grad_kn = kept[h, kind, 0] + from_x[h, kind, 0].astype(F32)
            grad_v = kept[h, kind, 1] + from_x[h, kind, 1].astype(F32)
            raw = k_ref[rows, cols].astype(F32)
            gk_ref[rows, cols] = norm_backward(
                raw, inverse_norm(raw), kgain_ref[...], grad_kn
            ).astype(BF16)
            gv_ref[rows, cols] = grad_v.astype(BF16)

    def reduce_sent(h):
        r_core(h).wait_send()
        for copy in r_far(h) + r_near(h):
            copy.wait_send()
        r_x(h).wait_send()

    for h in range(HK):
        gather_a(h)

    def prepare(h):
        for start, count, at in SEGMENTS:
            for g in range(GQ):
                cols = pl.ds(pl.multiple_of(h * GQ * DH + g * DH, DH), DH)
                rows = slice(start, start + count)
                dst = slice(at + g * count, at + (g + 1) * count)
                raw = q_ref[rows, cols].astype(F32)
                qn[h, dst, :] = (raw * inverse_norm(raw) * qgain_ref[...]).astype(BF16)
                grads = u_ref[rows, cols]
                if start == R_DEV + B_DEV:
                    ids = lax.broadcasted_iota(jnp.int32, (count, DH), 0)
                    grads = jnp.where(ids < leaf_length, grads.astype(F32), 0.0).astype(BF16)
                up[h, dst, :] = grads

    prepare(0)
    gather_b(0)
    prepare(1)
    gather_c(0)
    prepare(2)
    gather_d(0)
    prepare(3)
    gather_e(0)
    gain_part[...] = jnp.zeros_like(gain_part)

    def one_head(h, carry):
        for t in range(2):
            picked = kv[h, 1, t, 0:SPAN, :]
            for b in range(1, 4):
                picked = lax.select_n(
                    parent == b, picked, kv[h, 1, t, b * SPAN : (b + 1) * SPAN, :]
                )
            side[t, 0:SPAN, :] = picked
            side[t, SPAN : SPAN + L_DEV, :] = leaf_kv[h, t]
            side[t, SPAN + L_DEV :, :] = kv[
                h, 1, t, pl.ds(pl.multiple_of(own_branch * SPAN, SPAN), SPAN), :
            ]

        def scores_of(rb):
            rows = slice(rb * RB, (rb + 1) * RB)
            queries = qn[h, rows, :]
            upstream = up[h, rows, :]

            def chunk(keys, values, dst, allowed):
                count = keys.shape[0]
                e = jnp.exp2(dot(keys, queries, NT) * EXP2_SCALE)
                if allowed is not None:
                    e = jnp.where(allowed, e, 0.0)
                gp = dot(values, upstream, NT)
                expo[dst : dst + count, rows] = e.astype(BF16)
                gprobs[dst : dst + count, rows] = gp
                return fold(e), fold(e * gp)

            def key_ids(count):
                return lax.broadcasted_iota(jnp.int32, (count, RB), 0)

            def row_ids(count, first, period):
                return (lax.broadcasted_iota(jnp.int32, (count, RB), 1) + first) % period

            found = []
            for n in range(N_ROOT // SPAN):
                keys = slice(n * SPAN, (n + 1) * SPAN)
                allowed = None
                if rb == 0:
                    allowed = key_ids(SPAN) + n * SPAN <= row_ids(SPAN, 0, R_DEV) + me * R_DEV
                found.append(chunk(kv[h, 0, 0, keys, :], kv[h, 0, 1, keys, :], n * SPAN, allowed))
            if rb == 1:
                allowed = key_ids(SPAN) <= row_ids(SPAN, 0, B_DEV) + (me % 4) * B_DEV
                own_keys = slice(SPAN + L_DEV, 2 * SPAN + L_DEV)
                found.append(chunk(side[0, own_keys, :], side[1, own_keys, :], N_ROOT, allowed))
            if rb >= 2:
                found.append(chunk(side[0, :SPAN, :], side[1, :SPAN, :], N_ROOT, None))
                ids = key_ids(L_DEV)
                allowed = (ids <= row_ids(L_DEV, (rb - 2) * RB, L_DEV)) & (ids < leaf_length)
                leaf_keys = slice(SPAN, SPAN + L_DEV)
                found.append(
                    chunk(side[0, leaf_keys, :], side[1, leaf_keys, :], N_ROOT + SPAN, allowed)
                )
            total = jnp.sum(sum(f[0] for f in found), axis=0, keepdims=True)
            weighted = jnp.sum(sum(f[1] for f in found), axis=0, keepdims=True)
            inverse = 1.0 / total
            dot_rows[:, rows] = jnp.broadcast_to(weighted * inverse, (8, RB))
            spread = jnp.transpose(jnp.broadcast_to(inverse, (DH, RB)))
            inv_rows[rows, :] = spread
            q_scaled[rows, :] = (queries.astype(F32) * (spread * SCALE)).astype(BF16)
            up_scaled[rows, :] = (upstream.astype(F32) * spread).astype(BF16)

        def key_grads(keys, rows):
            gs = (
                expo[keys, rows].astype(F32) * (gprobs[keys, rows] - dot_rows[0:1, rows])
            ).astype(BF16)
            gscores[keys, rows] = gs
            return (
                dot(gs, q_scaled[rows, :], NN),
                dot(expo[keys, rows], up_scaled[rows, :], NN),
            )

        def gain_term(grad_kn, keys):
            return fold(grad_kn * keys.astype(F32))

        def root_grads(n):
            keys = slice(n * SPAN, (n + 1) * SPAN)
            grads = key_grads(keys, slice(0, Q_ROWS))
            gain_part[0:8] += gain_term(grads[0], kv[h, 0, 0, keys, :])
            for q in range(4):
                owner = 4 * n + q
                for t in range(2):
                    parts[h, owner % 2, (owner // 2) % 4, owner // 8, 0, t] = grads[t][
                        q * R_DEV : (q + 1) * R_DEV
                    ].astype(BF16)

        def side_grads():
            leaf_rows = slice(LEAF_AT, Q_ROWS)
            grads = key_grads(slice(N_ROOT, N_ROOT + SPAN + L_DEV), leaf_rows)
            gain_part[0:8] += gain_term(grads[0], side[0, : SPAN + L_DEV, :])
            cols = pl.ds(pl.multiple_of(h * DH, DH), DH)
            rows = slice(R_DEV + B_DEV, ROWS)
            raw = k_ref[rows, cols].astype(F32)
            gk_ref[rows, cols] = norm_backward(
                raw, inverse_norm(raw), kgain_ref[...], grads[0][SPAN:]
            ).astype(BF16)
            gv_ref[rows, cols] = grads[1][SPAN:].astype(BF16)
            own_grads = key_grads(slice(N_ROOT, N_ROOT + SPAN), slice(GQ * R_DEV, LEAF_AT))
            gain_part[0:8] += gain_term(own_grads[0], side[0, SPAN + L_DEV :, :])
            for b in range(4):
                to_parent = jnp.where(parent == b, 1.0, 0.0)
                to_own = jnp.where(own_branch == b, 1.0, 0.0)
                for t in range(2):
                    both = grads[t][:SPAN] * to_parent + own_grads[t] * to_own
                    for q in range(4):
                        owner = 4 * b + q
                        parts[h, owner % 2, (owner // 2) % 4, owner // 8, 1, t] = both[
                            q * B_DEV : (q + 1) * B_DEV
                        ].astype(BF16)

        def query_grads(rb):
            rows = slice(rb * RB, (rb + 1) * RB)
            grads = dot(gscores[:N_ROOT, rows], kv[h, 0, 0], TN)
            if rb == 1:
                grads += dot(gscores[N_ROOT : N_ROOT + SPAN, rows], side[0, SPAN + L_DEV :, :], TN)
            if rb >= 2:
                grads += dot(gscores[N_ROOT:, rows], side[0, : SPAN + L_DEV, :], TN)
            grad_qn[rows, :] = grads * (inv_rows[rows, :] * SCALE)

        def finish_queries():
            for start, count, at in SEGMENTS:
                for g in range(GQ):
                    cols = pl.ds(pl.multiple_of(h * GQ * DH + g * DH, DH), DH)
                    rows = slice(start, start + count)
                    grads = grad_qn[at + g * count : at + (g + 1) * count, :]
                    raw = q_ref[rows, cols].astype(F32)
                    inverse = inverse_norm(raw)
                    gq_ref[rows, cols] = norm_backward(
                        raw, inverse, qgain_ref[...], grads
                    ).astype(BF16)
                    gain_part[8:16] += fold(grads * raw * inverse)

        scores_of(0)
        pl.when(h < HK - 1)(lambda: gather_b(h + 1))
        scores_of(1)
        scores_of(2)
        pl.when(h < HK - 1)(lambda: gather_c(h + 1))
        pl.when(h > 0)(lambda: reduce_a(h - 1))
        pl.when(h > 1)(lambda: reduce_c(h - 2))
        scores_of(3)
        scores_of(4)
        pl.when(h < HK - 1)(lambda: gather_d(h + 1))
        for n in range(4):
            root_grads(n)
        side_grads()
        r_core(h).start()
        pl.when(h > 0)(lambda: reduce_b(h - 1))
        for rb in range(5):
            query_grads(rb)
        finish_queries()
        pl.when(h < HK - 1)(lambda: gather_e(h + 1))
        pl.when(h > 1)(lambda: reduce_d(h - 2))
        return carry

    lax.fori_loop(0, HK, one_head, 0)

    def a_copy(step, target):
        return pltpu.make_async_remote_copy(
            src_ref=gain_seq.at[0],
            dst_ref=gain_seq.at[step],
            send_sem=a_send.at[step],
            recv_sem=a_recv.at[step],
            device_id=(me_leaf, target),
            device_id_type=MESH,
        )

    def b_copy(step, target):
        return pltpu.make_async_remote_copy(
            src_ref=gain_leaf.at[0],
            dst_ref=gain_leaf.at[step],
            send_sem=b_send.at[step],
            recv_sem=b_recv.at[step],
            device_id=(target, me),
            device_id_type=MESH,
        )

    def a_start(step, carry):
        a_copy(step, (me + step) % N_SEQ).start()
        return carry

    def b_start(step, carry):
        b_copy(step, (me_leaf + step) % n_leaf).start()
        return carry

    def a_wait(step, total):
        a_copy(step, (me + step) % N_SEQ).wait()
        return total + gain_seq[step]

    def b_wait(step, total):
        b_copy(step, (me_leaf + step) % n_leaf).wait()
        return total + gain_leaf[step]

    row = lax.broadcasted_iota(jnp.int32, (8, DH), 0)
    key_sum = jnp.sum(gain_part[0:8], axis=0, keepdims=True) / kgain_ref[...]
    query_sum = jnp.sum(gain_part[8:16], axis=0, keepdims=True)
    gain_seq[0] = jnp.where(row == 0, query_sum, key_sum)
    lax.fori_loop(1, N_SEQ, a_start, 0)
    reduce_a(HK - 1)
    reduce_c(HK - 2)
    gain_leaf[0] = lax.fori_loop(1, N_SEQ, a_wait, gain_seq[0])
    lax.fori_loop(1, n_leaf, b_start, 0)
    reduce_b(HK - 1)
    reduce_d(HK - 2)
    gains_ref[...] = lax.fori_loop(1, n_leaf, b_wait, gain_leaf[0])
    reduce_c(HK - 1)
    reduce_d(HK - 1)
    for h in range(HK):
        gather_sent(h)
        reduce_sent(h)


def on_device(
    query_raw, key_raw, value_raw, grad_out, query_gain, key_gain, leaf_parent, leaf_blocks
):
    n_leaf = lax.axis_size("leaf")
    vmem = pl.BlockSpec(memory_space=pltpu.VMEM)
    smem = pl.BlockSpec(memory_space=pltpu.SMEM)
    keys = N_ROOT + SPAN + L_DEV
    dma = pltpu.SemaphoreType.DMA
    grad_query, grad_key, grad_value, gains = pl.pallas_call(
        functools.partial(kernel, n_leaf),
        out_shape=(
            jax.ShapeDtypeStruct((ROWS, HQ * DH), BF16),
            jax.ShapeDtypeStruct((ROWS, HK * DH), BF16),
            jax.ShapeDtypeStruct((ROWS, HK * DH), BF16),
            jax.ShapeDtypeStruct((8, DH), F32),
        ),
        in_specs=[smem, smem] + [vmem] * 6,
        out_specs=(vmem,) * 4,
        scratch_shapes=[
            pltpu.VMEM((HK, 2, 2, N_ROOT, DH), BF16),
            pltpu.VMEM((HK, 2, L_DEV, DH), BF16),
            pltpu.VMEM((2, 2 * SPAN + L_DEV, DH), BF16),
            pltpu.VMEM((HK, Q_ROWS, DH), BF16),
            pltpu.VMEM((HK, Q_ROWS, DH), BF16),
            pltpu.VMEM((keys, Q_ROWS), BF16),
            pltpu.VMEM((keys, Q_ROWS), F32),
            pltpu.VMEM((keys, Q_ROWS), BF16),
            pltpu.VMEM((Q_ROWS, DH), BF16),
            pltpu.VMEM((Q_ROWS, DH), BF16),
            pltpu.VMEM((Q_ROWS, DH), F32),
            pltpu.VMEM((8, Q_ROWS), F32),
            pltpu.VMEM((Q_ROWS, DH), F32),
            pltpu.VMEM((HK, 2, 4, 2, 2, 2, R_DEV, DH), BF16),
            pltpu.VMEM((HK, 4, 2, 2, 2, R_DEV, DH), BF16),
            pltpu.VMEM((HK, 2, 2, 2, R_DEV, DH), BF16),
            pltpu.VMEM((HK, 2, 2, 2, 2, R_DEV, DH), BF16),
            pltpu.VMEM((HK, 2, 2, R_DEV, DH), BF16),
            pltpu.VMEM((HK, 2, 2, R_DEV, DH), F32),
            pltpu.VMEM((HK, 2, 2, R_DEV, DH), BF16),
            pltpu.VMEM((16, DH), F32),
            pltpu.VMEM((N_SEQ, 8, DH), F32),
            pltpu.VMEM((n_leaf, 8, DH), F32),
            dma((HK, N_G)),
            dma((HK, N_G)),
            dma((HK, N_R)),
            dma((HK, N_R)),
            dma((N_SEQ,)),
            dma((N_SEQ,)),
            dma((n_leaf,)),
            dma((n_leaf,)),
        ],
        compiler_params=pltpu.CompilerParams(
            collective_id=0, has_side_effects=True, vmem_limit_bytes=60 * 2**20
        ),
        name="attention_backward",
    )(
        leaf_parent,
        leaf_blocks,
        query_raw[0],
        key_raw[0],
        value_raw[0],
        grad_out[0],
        query_gain.reshape(1, DH),
        key_gain.reshape(1, DH),
    )
    return grad_query[None], grad_key[None], grad_value[None], gains[0], gains[1]


def solution(mesh):
    return jax.shard_map(
        on_device,
        mesh=mesh,
        in_specs=(
            P("leaf", "seq", None),
            P("leaf", "seq", None),
            P("leaf", "seq", None),
            P("leaf", "seq", None),
            P(),
            P(),
            P("leaf", "seq"),
            P("leaf", "seq"),
        ),
        out_specs=(
            P("leaf", "seq", None),
            P("leaf", "seq", None),
            P("leaf", "seq", None),
            P(),
            P(),
        ),
        check_vma=False,
    )
```

time: 661 us -> 95.9 us (0.15); the launches traced: 648 us -> 95.7 us
  waiting for transfers between devices: 257 us -> 0 us
  matrix products: 124 us -> 0 us
  local copies, waits for them, and re-layouts: 127 us -> 5.31 us
  Pallas kernels: 0 us -> 88.5 us
  blocking collectives: 74.2 us -> 0 us
  other arithmetic: 47.9 us -> 0 us
  between operations: 16.7 us -> 1.94 us
    all_gather x4 -> x0, waiting for transfers between devices: 145 us -> none  [the longest x1 48.5 us: on_device(): lax.all_gather(values_loc[R_DEV:R_DEV + B_DEV], 'seq', axis=0, tiled=True)]
    dot_general x112 -> x0, matrix products: 124 us -> none  [contract(): return jnp.einsum(form, left, right, preferred_element_type=jnp.float32)]
    reduce_scatter x4 -> x0, waiting for transfers between devices: 111 us -> none  [the longest x1 81.6 us: on_device(): lax.psum_scatter(part_v, 'seq', scatter_dimension=0, tiled=True)]
    pallas_call x0 -> x1, Pallas kernels: none -> 88.5 us  [on_device(): pl.pallas_call(functools.partial(kernel, n_leaf), out_shape=(jax.ShapeDty...]
    psum x1 -> x0, blocking collectives: 74.2 us -> none  [on_device(): lax.psum((query_gain_part, key_gain_part), ('leaf', 'seq'))]
    unnamed x109 -> x7, local copies, waits for them, and re-layouts: 23.6 us -> 4.04 us
    dynamic_update_slice x34 -> x0, local copies, waits for them, and re-layouts: 14.3 us -> none  [the longest x32 11.2 us: set_forward(): return lax.map(one_head, (query_h, keys_h, values_h))]
    mul x10 -> x0, local copies, waits for them, and re-layouts: 13.9 us -> none  [the longest x4 6.36 us: norm_backward(): values * inverse * inverse * inverse]
  transfers between devices with their start and end apart: 8 -> 0, of which waited for: 7 -> 0; matrix products, arithmetic and copies ran while one was open for 29% -> 0% of each run, Pallas kernels for 0% -> 0%
where the time goes in v1:
time: 95.9 us; the launch traced here: 95.7 us
  Pallas kernels  88.5 us (92%)
  local copies, waits for them, and re-layouts  5.31 us (6%)
  between operations  1.94 us (2%)
    pallas_call x1, Pallas kernels, on_device(): pl.pallas_call(functools.partial(kernel, n_leaf), out_shape=(jax.ShapeDty...  88.5 us
    unnamed x7, local copies, waits for them, and re-layouts  4.04 us

profile of v1, /device:TPU:8, one launch (start us, length us, event | category | flops | bytes accessed | tf_op | source)
XLA Modules:
  0.0 95.7 jit_solution(1328609162346482790)
XLA Ops:
  1.9 88.5 %attention_backward.1 = (bf16[320,2048]{1,0:T(8,128)(2,1)}, bf16[320,512]{1,0:T(8,128)(2,1)}, bf16[320,512]{1,0:T(8,128)(2,1)}, f32[8,128]{1,0:T(8,128)}) custom-call(s32[1,1]{1,0:T(1,128)S(6)} %copy.16.parent_ref, s32[1,1]{1,0:T(1,128)S(6)} %copy.17.blocks_ref, bf16[320,2048]{1,0:T(8,128)(2,1)} %bitcast.13, bf16[320,512]{1,0:T(8,128)(2,1)} %bitcast.18, ...), custom_call_target="tpu_custom_call" | custom-call | tf_op jit(solution)/shard_map/attention_backward/pallas_call | solution.py:549
  90.4 1.3 %slice_bitcast_fusion = (f32[128]{0:T(128)}, f32[128]{0:T(128)}) fusion(f32[8,128]{1,0:T(8,128)} %get-tuple-element.12), kind=kLoop, calls=%fused_computation | loop fusion | bytes 2048 | tf_op jit(solution)/shard_map/squeeze | solution.py:606
  91.7 0.0 copy-start.1
  91.7 0.0 copy-start
  91.7 2.6 %copy.18 = bf16[1,320,2048]{2,1,0:T(8,128)(2,1)} copy(bf16[1,320,2048]{2,1,0:T(8,128)(2,1)} %bitcast.15) | data formatting | bytes 2621440
  94.3 0.0 copy-done.1
  94.3 0.7 copy.19
  95.0 0.0 copy-done
  95.0 0.7 copy.20
Async XLA Ops:
  91.7 2.6 %copy-start.1 = (bf16[320,512]{1,0:T(8,128)(2,1)S(1)}, bf16[320,512]{1,0:T(8,128)(2,1)}, u32[]{:S(2)}) copy-start(bf16[320,512]{1,0:T(8,128)(2,1)} %get-tuple-element.10) | copy-start | bytes 983044
  91.7 3.3 %copy-start = (bf16[320,512]{1,0:T(8,128)(2,1)S(1)}, bf16[320,512]{1,0:T(8,128)(2,1)}, u32[]{:S(2)}) copy-start(bf16[320,512]{1,0:T(8,128)(2,1)} %get-tuple-element.11) | copy-start | bytes 983044

commit v2 on v1

v2 whole, which is shorter than its diff:
```python
import functools
import math

import jax
import jax.numpy as jnp
from jax import lax
from jax.experimental import pallas as pl
from jax.experimental.pallas import tpu as pltpu
from jax.sharding import PartitionSpec as P

HQ = 16
HK = 4
DH = 128
GQ = HQ // HK
R_DEV = 64
B_DEV = 64
LEAF_BLOCK = 64
L_DEV = 192
ROWS = 320
N_SEQ = 16
N_ROOT = R_DEV * N_SEQ
SPAN = 256
RB = 256
Q_ROWS = ROWS * GQ
LEAF_AT = GQ * (R_DEV + B_DEV)
EPS = 1e-06
SCALE = 1.0 / math.sqrt(DH)
EXP2_SCALE = SCALE / math.log(2.0)

F32 = jnp.float32
BF16 = jnp.bfloat16
MESH = pl.DeviceIdType.MESH
NT = (((1,), (1,)), ((), ()))
NN = (((1,), (0,)), ((), ()))
TN = (((0,), (0,)), ((), ()))

SEGMENTS = ((0, R_DEV, 0), (R_DEV, B_DEV, GQ * R_DEV), (R_DEV + B_DEV, L_DEV, LEAF_AT))

CHIPS = 8
HALVES = 2 * HK


def dot(left, right, dims):
    return lax.dot_general(left, right, dims, preferred_element_type=F32)


def inverse_norm(values):
    return lax.rsqrt(jnp.mean(values * values, axis=-1, keepdims=True) + EPS)


def norm_backward(values, inverse, gain, upstream):
    scaled = upstream * gain
    mean = jnp.mean(scaled * values, axis=-1, keepdims=True)
    return inverse * scaled - values * (inverse * inverse * inverse * mean)


def fold(array):
    return jnp.sum(array.reshape(array.shape[0] // 8, 8, array.shape[1]), axis=0)


def kernel(
    n_leaf,
    parent_ref,
    blocks_ref,
    q_hbm,
    k_ref,
    v_ref,
    u_hbm,
    qgain_ref,
    kgain_ref,
    gq_hbm,
    gk_ref,
    gv_ref,
    gains_ref,
    q_ref,
    u_ref,
    gq_ref,
    kv,
    leaf_kv,
    side,
    qn,
    up,
    expo,
    gprobs,
    gscores,
    q_scaled,
    up_scaled,
    inv_rows,
    dot_rows,
    sums,
    grad_qn,
    parts,
    from_core,
    from_chip,
    gain_part,
    gain_seq,
    gain_leaf,
    g_send,
    g_recv,
    r_send,
    r_recv,
    a_send,
    a_recv,
    b_send,
    b_recv,
    io_sem,
):
    me = lax.axis_index("seq")
    me_leaf = lax.axis_index("leaf")
    x = me // 8
    y = (me // 2) % 4
    c = me % 2
    def place(px, py, pc):
        return px * 8 + py * 2 + pc

    dev_core = place(x, y, 1 - c)
    parent = parent_ref[0, 0]
    leaf_length = blocks_ref[0, 0] * LEAF_BLOCK
    own_branch = me // 4

    load_q = pltpu.make_async_copy(q_hbm, q_ref, io_sem.at[HK])
    load_u = pltpu.make_async_copy(u_hbm, u_ref, io_sem.at[HK + 1])

    barrier = pltpu.get_barrier_semaphore()

    def greet_seq(step, carry):
        pl.semaphore_signal(
            barrier, inc=1, device_id=(me_leaf, (me + step) % N_SEQ), device_id_type=MESH
        )
        return carry

    def greet_leaf(step, carry):
        pl.semaphore_signal(
            barrier, inc=1, device_id=((me_leaf + step) % n_leaf, me), device_id_type=MESH
        )
        return carry

    lax.fori_loop(1, N_SEQ, greet_seq, 0)
    lax.fori_loop(1, n_leaf, greet_leaf, 0)

    load_q.start()
    load_u.start()


    def prepare_keys(h):
        cols = slice(h * DH, (h + 1) * DH)
        raw = k_ref[:, cols].astype(F32)
        normed = (raw * inverse_norm(raw) * kgain_ref[...]).astype(BF16)
        values = v_ref[:, cols]
        kv[h, 0, 0, x, y, c] = normed[:R_DEV]
        kv[h, 1, 0, x, y, c] = normed[R_DEV : R_DEV + B_DEV]
        leaf_kv[h, 0] = normed[R_DEV + B_DEV :]
        kv[h, 0, 1, x, y, c] = values[:R_DEV]
        kv[h, 1, 1, x, y, c] = values[R_DEV : R_DEV + B_DEV]
        leaf_kv[h, 1] = values[R_DEV + B_DEV :]

    prepare_keys(0)
    pl.semaphore_wait(barrier, N_SEQ - 1 + n_leaf - 1)

    def chip_at(number, sign):
        other = number // 4
        return x + other * (1 - 2 * x), (y + sign * (number % 4)) % 4

    def g_copy(half, number, px, py, target):
        ref = kv.at[half // 2, half % 2, :, px, py, c]
        return pltpu.make_async_remote_copy(
            src_ref=ref,
            dst_ref=ref,
            send_sem=g_send.at[half, number],
            recv_sem=g_recv.at[half, number],
            device_id=(me_leaf, target),
            device_id_type=MESH,
        )

    def g_core(half, core):
        ref = kv.at[half // 2, half % 2, :, :, :, core]
        return pltpu.make_async_remote_copy(
            src_ref=ref,
            dst_ref=ref,
            send_sem=g_send.at[half, 0],
            recv_sem=g_recv.at[half, 0],
            device_id=(me_leaf, dev_core),
            device_id_type=MESH,
        )

    def gather_a(half):
        for number in range(1, CHIPS):
            px, py = chip_at(number, 1)
            g_copy(half, number, x, y, place(px, py, c)).start()

    def gather_b(half):
        for number in range(1, CHIPS):
            px, py = chip_at(number, 3)
            g_copy(half, number, px, py, place(px, py, c)).wait_recv()
        g_core(half, c).start()

    def gather_c(half):
        g_core(half, 1 - c).wait_recv()

    def gather_sent(half):
        for number in range(1, CHIPS):
            px, py = chip_at(number, 1)
            g_copy(half, number, x, y, place(px, py, c)).wait_send()
        g_core(half, c).wait_send()

    def r_core(half):
        return pltpu.make_async_remote_copy(
            src_ref=parts.at[half, 1 - c],
            dst_ref=from_core.at[half],
            send_sem=r_send.at[half, 0],
            recv_sem=r_recv.at[half, 0],
            device_id=(me_leaf, dev_core),
            device_id_type=MESH,
        )

    def r_copy(half, number):
        px, py = chip_at(number, 1)
        return pltpu.make_async_remote_copy(
            src_ref=parts.at[half, c, px, py],
            dst_ref=from_chip.at[half, number],
            send_sem=r_send.at[half, number],
            recv_sem=r_recv.at[half, number],
            device_id=(me_leaf, place(px, py, c)),
            device_id_type=MESH,
        )

    def reduce_a(half):
        r_core(half).wait_recv()
        for px in range(2):
            for py in range(4):
                parts[half, c, px, py] = (
                    parts[half, c, px, py].astype(F32) + from_core[half, px, py].astype(F32)
                ).astype(BF16)
        for number in range(1, CHIPS):
            r_copy(half, number).start()

    def reduce_b(half):
        for number in range(1, CHIPS):
            r_copy(half, number).wait_recv()
        total = parts[half, c, x, y].astype(F32)
        for number in range(1, CHIPS):
            total += from_chip[half, number].astype(F32)
        cols = pl.ds(pl.multiple_of((half // 2) * DH, DH), DH)
        rows = pl.ds(pl.multiple_of((half % 2) * R_DEV, R_DEV), R_DEV)
        raw = k_ref[rows, cols].astype(F32)
        gk_ref[rows, cols] = norm_backward(
            raw, inverse_norm(raw), kgain_ref[...], total[0]
        ).astype(BF16)
        gv_ref[rows, cols] = total[1].astype(BF16)

    def reduce_sent(half):
        r_core(half).wait_send()
        for number in range(1, CHIPS):
            r_copy(half, number).wait_send()

    def prepare(h):
        for start, count, at in SEGMENTS:
            for g in range(GQ):
                cols = pl.ds(pl.multiple_of(h * GQ * DH + g * DH, DH), DH)
                rows = slice(start, start + count)
                dst = slice(at + g * count, at + (g + 1) * count)
                raw = q_ref[rows, cols].astype(F32)
                qn[h, dst, :] = (raw * inverse_norm(raw) * qgain_ref[...]).astype(BF16)
                grads = u_ref[rows, cols]
                if start == R_DEV + B_DEV:
                    ids = lax.broadcasted_iota(jnp.int32, (count, DH), 0)
                    grads = jnp.where(ids < leaf_length, grads.astype(F32), 0.0).astype(BF16)
                up[h, dst, :] = grads

    for half in range(2):
        gather_a(half)
    for h in range(1, HK):
        prepare_keys(h)
    for half in range(2, HALVES):
        gather_a(half)
    load_q.wait()
    load_u.wait()
    for h in range(HK):
        prepare(h)
    gather_b(0)
    gather_b(1)
    gather_c(0)
    gain_part[...] = jnp.zeros_like(gain_part)

    def one_head(h, carry):
        def pick_side():
            for t in range(2):
                picked = kv[h, 1, t, 0, 0:2].reshape(SPAN, DH)
                for b in range(1, 4):
                    picked = lax.select_n(
                        parent == b,
                        picked,
                        kv[h, 1, t, b // 2, b % 2 * 2 : b % 2 * 2 + 2].reshape(SPAN, DH),
                    )
                side[h, t, 0:SPAN, :] = picked
                side[h, t, SPAN : SPAN + L_DEV, :] = leaf_kv[h, t]
                side[h, t, SPAN + L_DEV :, :] = kv[h, 1, t, x, pl.ds(y // 2 * 2, 2)].reshape(
                    SPAN, DH
                )

        def key_ids(count):
            return lax.broadcasted_iota(jnp.int32, (count, RB), 0)

        def row_ids(count, first, period):
            return (lax.broadcasted_iota(jnp.int32, (count, RB), 1) + first) % period

        def chunk(rb, keys, values, dst, allowed):
            rows = slice(rb * RB, (rb + 1) * RB)
            count = keys.shape[0]
            e = jnp.exp2(dot(keys, qn[h, rows, :], NT) * EXP2_SCALE)
            if allowed is not None:
                e = jnp.where(allowed, e, 0.0)
            gp = dot(values, up[h, rows, :], NT)
            expo[dst : dst + count, rows] = e.astype(BF16)
            gprobs[dst : dst + count, rows] = gp
            return fold(e), fold(e * gp)

        def root_block(t, n):
            return kv[h, 0, t, n // 2, n % 2 * 2 : n % 2 * 2 + 2].reshape(SPAN, DH)

        def root_scores(rb):
            found = []
            for n in range(N_ROOT // SPAN):
                allowed = None
                if rb == 0:
                    allowed = key_ids(SPAN) + n * SPAN <= row_ids(SPAN, 0, R_DEV) + me * R_DEV
                found.append(chunk(rb, root_block(0, n), root_block(1, n), n * SPAN, allowed))
            rows = slice(rb * RB, (rb + 1) * RB)
            sums[0, :, rows] = sum(f[0] for f in found)
            sums[1, :, rows] = sum(f[1] for f in found)

        def side_scores(rb):
            rows = slice(rb * RB, (rb + 1) * RB)
            found = [(sums[0, :, rows], sums[1, :, rows])]
            if rb == 1:
                allowed = key_ids(SPAN) <= row_ids(SPAN, 0, B_DEV) + (me % 4) * B_DEV
                keys = slice(SPAN + L_DEV, 2 * SPAN + L_DEV)
                found.append(chunk(rb, side[h, 0, keys, :], side[h, 1, keys, :], N_ROOT, allowed))
            if rb >= 2:
                found.append(
                    chunk(rb, side[h, 0, :SPAN, :], side[h, 1, :SPAN, :], N_ROOT, None)
                )
                ids = key_ids(L_DEV)
                allowed = (ids <= row_ids(L_DEV, (rb - 2) * RB, L_DEV)) & (ids < leaf_length)
                keys = slice(SPAN, SPAN + L_DEV)
                found.append(
                    chunk(rb, side[h, 0, keys, :], side[h, 1, keys, :], N_ROOT + SPAN, allowed)
                )
            total = jnp.sum(sum(f[0] for f in found), axis=0, keepdims=True)
            weighted = jnp.sum(sum(f[1] for f in found), axis=0, keepdims=True)
            inverse = 1.0 / total
            dot_rows[:, rows] = jnp.broadcast_to(weighted * inverse, (8, RB))
            spread = jnp.transpose(jnp.broadcast_to(inverse, (DH, RB)))
            inv_rows[h, rows, :] = spread
            q_scaled[rows, :] = (qn[h, rows, :].astype(F32) * (spread * SCALE)).astype(BF16)
            up_scaled[rows, :] = (up[h, rows, :].astype(F32) * spread).astype(BF16)

        def key_grads(keys, rows):
            gs = (
                expo[keys, rows].astype(F32) * (gprobs[keys, rows] - dot_rows[0:1, rows])
            ).astype(BF16)
            gscores[h, keys, rows] = gs
            return (
                dot(gs, q_scaled[rows, :], NN),
                dot(expo[keys, rows], up_scaled[rows, :], NN),
            )

        def gain_term(grad_kn, keys):
            return fold(grad_kn * keys.astype(F32))

        def root_grads(n):
            keys = slice(n * SPAN, (n + 1) * SPAN)
            grads = key_grads(keys, slice(0, Q_ROWS))
            gain_part[0:8] += gain_term(grads[0], root_block(0, n))
            for q in range(4):
                owner = 4 * n + q
                for t in range(2):
                    parts[2 * h, owner % 2, owner // 8, (owner // 2) % 4, t] = grads[t][
                        q * R_DEV : (q + 1) * R_DEV
                    ].astype(BF16)

        def side_grads():
            leaf_rows = slice(LEAF_AT, Q_ROWS)
            grads = key_grads(slice(N_ROOT, N_ROOT + SPAN + L_DEV), leaf_rows)
            gain_part[0:8] += gain_term(grads[0], side[h, 0, : SPAN + L_DEV, :])
            cols = pl.ds(pl.multiple_of(h * DH, DH), DH)
            rows = slice(R_DEV + B_DEV, ROWS)
            raw = k_ref[rows, cols].astype(F32)
            gk_ref[rows, cols] = norm_backward(
                raw, inverse_norm(raw), kgain_ref[...], grads[0][SPAN:]
            ).astype(BF16)
            gv_ref[rows, cols] = grads[1][SPAN:].astype(BF16)
            own_grads = key_grads(slice(N_ROOT, N_ROOT + SPAN), slice(GQ * R_DEV, LEAF_AT))
            gain_part[0:8] += gain_term(own_grads[0], side[h, 0, SPAN + L_DEV :, :])
            for b in range(4):
                to_parent = jnp.where(parent == b, 1.0, 0.0)
                to_own = jnp.where(own_branch == b, 1.0, 0.0)
                for t in range(2):
                    both = grads[t][:SPAN] * to_parent + own_grads[t] * to_own
                    for q in range(4):
                        owner = 4 * b + q
                        parts[2 * h + 1, owner % 2, owner // 8, (owner // 2) % 4, t] = both[
                            q * B_DEV : (q + 1) * B_DEV
                        ].astype(BF16)

        for rb in range(5):
            root_scores(rb)

        @pl.when(h < HK - 1)
        def _():
            gather_b(2 * h + 2)
            gather_b(2 * h + 3)

        @pl.when(h > 0)
        def _():
            reduce_a(2 * h - 2)
            reduce_a(2 * h - 1)

        @pl.when(h > 1)
        def _():
            reduce_b(2 * h - 4)
            reduce_b(2 * h - 3)

        gather_c(2 * h + 1)
        pick_side()
        for rb in range(5):
            side_scores(rb)
        for n in range(4):
            root_grads(n)
        r_core(2 * h).start()
        side_grads()
        r_core(2 * h + 1).start()

        @pl.when(h < HK - 1)
        def _():
            gather_c(2 * h + 2)

        return carry

    lax.fori_loop(0, HK, one_head, 0)

    def store_q(h):
        cols = pl.ds(h * GQ * DH, GQ * DH)
        return pltpu.make_async_copy(gq_ref.at[:, cols], gq_hbm.at[:, cols], io_sem.at[h])

    def queries_of(h):
        def query_grads(rb):
            rows = slice(rb * RB, (rb + 1) * RB)
            grads = dot(gscores[h, :N_ROOT, rows], kv[h, 0, 0].reshape(N_ROOT, DH), TN)
            if rb == 1:
                grads += dot(gscores[h, N_ROOT : N_ROOT + SPAN, rows], side[h, 0, SPAN + L_DEV :, :], TN)
            if rb >= 2:
                grads += dot(gscores[h, N_ROOT:, rows], side[h, 0, : SPAN + L_DEV, :], TN)
            grad_qn[rows, :] = grads * (inv_rows[h, rows, :] * SCALE)

        def finish_queries():
            for start, count, at in SEGMENTS:
                for g in range(GQ):
                    cols = pl.ds(pl.multiple_of(h * GQ * DH + g * DH, DH), DH)
                    rows = slice(start, start + count)
                    grads = grad_qn[at + g * count : at + (g + 1) * count, :]
                    raw = q_ref[rows, cols].astype(F32)
                    inverse = inverse_norm(raw)
                    gq_ref[rows, cols] = norm_backward(
                        raw, inverse, qgain_ref[...], grads
                    ).astype(BF16)
                    gain_part[8:16] += fold(grads * raw * inverse)

        for rb in range(5):
            query_grads(rb)
        finish_queries()
        store_q(h).start()

    def a_copy(step, target):
        return pltpu.make_async_remote_copy(
            src_ref=gain_seq.at[0],
            dst_ref=gain_seq.at[step],
            send_sem=a_send.at[step],
            recv_sem=a_recv.at[step],
            device_id=(me_leaf, target),
            device_id_type=MESH,
        )

    def b_copy(step, target):
        return pltpu.make_async_remote_copy(
            src_ref=gain_leaf.at[0],
            dst_ref=gain_leaf.at[step],
            send_sem=b_send.at[step],
            recv_sem=b_recv.at[step],
            device_id=(target, me),
            device_id_type=MESH,
        )

    def a_start(step, carry):
        a_copy(step, (me + step) % N_SEQ).start()
        return carry

    def b_start(step, carry):
        b_copy(step, (me_leaf + step) % n_leaf).start()
        return carry

    def a_wait(step, total):
        a_copy(step, (me + step) % N_SEQ).wait()
        return total + gain_seq[step]

    def b_wait(step, total):
        b_copy(step, (me_leaf + step) % n_leaf).wait()
        return total + gain_leaf[step]

    root, branch = HALVES - 2, HALVES - 1
    reduce_a(root)
    queries_of(0)
    reduce_a(branch)
    queries_of(1)
    queries_of(2)
    reduce_b(root - 2)
    reduce_b(branch - 2)
    queries_of(3)
    row = lax.broadcasted_iota(jnp.int32, (8, DH), 0)
    key_sum = jnp.sum(gain_part[0:8], axis=0, keepdims=True) / kgain_ref[...]
    query_sum = jnp.sum(gain_part[8:16], axis=0, keepdims=True)
    gain_seq[0] = jnp.where(row == 0, query_sum, key_sum)
    lax.fori_loop(1, N_SEQ, a_start, 0)
    reduce_b(root)
    gain_leaf[0] = lax.fori_loop(1, N_SEQ, a_wait, gain_seq[0])
    lax.fori_loop(1, n_leaf, b_start, 0)
    reduce_b(branch)
    gains_ref[...] = lax.fori_loop(1, n_leaf, b_wait, gain_leaf[0])
    for half in range(HALVES):
        gather_sent(half)
        reduce_sent(half)
    for h in range(HK):
        store_q(h).wait()


def on_device(
    query_raw, key_raw, value_raw, grad_out, query_gain, key_gain, leaf_parent, leaf_blocks
):
    n_leaf = lax.axis_size("leaf")
    vmem = pl.BlockSpec(memory_space=pltpu.VMEM)
    smem = pl.BlockSpec(memory_space=pltpu.SMEM)
    hbm = pl.BlockSpec(memory_space=pl.ANY)
    keys = N_ROOT + SPAN + L_DEV
    dma = pltpu.SemaphoreType.DMA
    grad_query, grad_key, grad_value, gains = pl.pallas_call(
        functools.partial(kernel, n_leaf),
        out_shape=(
            jax.ShapeDtypeStruct((ROWS, HQ * DH), BF16),
            jax.ShapeDtypeStruct((ROWS, HK * DH), BF16),
            jax.ShapeDtypeStruct((ROWS, HK * DH), BF16),
            jax.ShapeDtypeStruct((8, DH), F32),
        ),
        in_specs=[smem, smem, hbm, vmem, vmem, hbm, vmem, vmem],
        out_specs=(hbm, vmem, vmem, vmem),
        scratch_shapes=[
            pltpu.VMEM((ROWS, HQ * DH), BF16),
            pltpu.VMEM((ROWS, HQ * DH), BF16),
            pltpu.VMEM((ROWS, HQ * DH), BF16),
            pltpu.VMEM((HK, 2, 2, 2, 4, 2, R_DEV, DH), BF16),
            pltpu.VMEM((HK, 2, L_DEV, DH), BF16),
            pltpu.VMEM((HK, 2, 2 * SPAN + L_DEV, DH), BF16),
            pltpu.VMEM((HK, Q_ROWS, DH), BF16),
            pltpu.VMEM((HK, Q_ROWS, DH), BF16),
            pltpu.VMEM((keys, Q_ROWS), BF16),
            pltpu.VMEM((keys, Q_ROWS), F32),
            pltpu.VMEM((HK, keys, Q_ROWS), BF16),
            pltpu.VMEM((Q_ROWS, DH), BF16),
            pltpu.VMEM((Q_ROWS, DH), BF16),
            pltpu.VMEM((HK, Q_ROWS, DH), F32),
            pltpu.VMEM((8, Q_ROWS), F32),
            pltpu.VMEM((2, 8, Q_ROWS), F32),
            pltpu.VMEM((Q_ROWS, DH), F32),
            pltpu.VMEM((HALVES, 2, 2, 4, 2, R_DEV, DH), BF16),
            pltpu.VMEM((HALVES, 2, 4, 2, R_DEV, DH), BF16),
            pltpu.VMEM((HALVES, CHIPS, 2, R_DEV, DH), BF16),
            pltpu.VMEM((16, DH), F32),
            pltpu.VMEM((N_SEQ, 8, DH), F32),
            pltpu.VMEM((n_leaf, 8, DH), F32),
            dma((HALVES, CHIPS)),
            dma((HALVES, CHIPS)),
            dma((HALVES, CHIPS)),
            dma((HALVES, CHIPS)),
            dma((N_SEQ,)),
            dma((N_SEQ,)),
            dma((n_leaf,)),
            dma((n_leaf,)),
            dma((HK + 2,)),
        ],
        compiler_params=pltpu.CompilerParams(
            collective_id=0, has_side_effects=True, vmem_limit_bytes=60 * 2**20
        ),
        name="attention_backward",
    )(
        leaf_parent,
        leaf_blocks,
        query_raw[0],
        key_raw[0],
        value_raw[0],
        grad_out[0],
        query_gain.reshape(1, DH),
        key_gain.reshape(1, DH),
    )
    return grad_query[None], grad_key[None], grad_value[None], gains[0], gains[1]


def solution(mesh):
    return jax.shard_map(
        on_device,
        mesh=mesh,
        in_specs=(
            P("leaf", "seq", None),
            P("leaf", "seq", None),
            P("leaf", "seq", None),
            P("leaf", "seq", None),
            P(),
            P(),
            P("leaf", "seq"),
            P("leaf", "seq"),
        ),
        out_specs=(
            P("leaf", "seq", None),
            P("leaf", "seq", None),
            P("leaf", "seq", None),
            P(),
            P(),
        ),
        check_vma=False,
    )
```

time: 95.9 us -> 79.6 us (0.83)
  Pallas kernels: 88.5 us -> 71.3 us
    pallas_call x1, Pallas kernels: 88.5 us -> 71.3 us  [on_device(): pl.pallas_call(functools.partial(kernel, n_leaf), out_shape=(jax.ShapeDty...]
where the time goes in v2:
time: 79.6 us; the launch traced here: 78.6 us
  Pallas kernels  71.3 us (90%)
  local copies, waits for them, and re-layouts  5.31 us (7%)
  between operations  1.94 us (2%)
    pallas_call x1, Pallas kernels, on_device(): pl.pallas_call(functools.partial(kernel, n_leaf), out_shape=(jax.ShapeDty...  71.3 us
    unnamed x7, local copies, waits for them, and re-layouts  4.04 us

profile of v2, /device:TPU:8, one launch (start us, length us, event | category | flops | bytes accessed | tf_op | source)
XLA Modules:
  0.0 78.6 jit_solution(3960516791690515524)
XLA Ops:
  1.9 71.3 %attention_backward.1 = (bf16[320,2048]{1,0:T(8,128)(2,1)}, bf16[320,512]{1,0:T(8,128)(2,1)}, bf16[320,512]{1,0:T(8,128)(2,1)}, f32[8,128]{1,0:T(8,128)}) custom-call(s32[1,1]{1,0:T(1,128)S(6)} %copy.16.parent_ref, s32[1,1]{1,0:T(1,128)S(6)} %copy.17.blocks_ref, bf16[320,2048]{1,0:T(8,128)(2,1)} %bitcast.13, bf16[320,512]{1,0:T(8,128)(2,1)} %bitcast.18, ...), custom_call_target="tpu_custom_call" | custom-call | tf_op jit(solution)/shard_map/attention_backward/pallas_call | solution.py:545
  73.3 1.3 %slice_bitcast_fusion = (f32[128]{0:T(128)}, f32[128]{0:T(128)}) fusion(f32[8,128]{1,0:T(8,128)} %get-tuple-element.12), kind=kLoop, calls=%fused_computation | loop fusion | bytes 2048 | tf_op jit(solution)/shard_map/squeeze | solution.py:603
  74.5 0.0 copy-start.1
  74.5 0.0 copy-start
  74.5 2.6 %copy.18 = bf16[1,320,2048]{2,1,0:T(8,128)(2,1)} copy(bf16[1,320,2048]{2,1,0:T(8,128)(2,1)} %bitcast.15) | data formatting | bytes 2621440
  77.1 0.0 copy-done.1
  77.1 0.7 copy.19
  77.8 0.0 copy-done
  77.8 0.7 copy.20
Async XLA Ops:
  74.5 2.6 %copy-start.1 = (bf16[320,512]{1,0:T(8,128)(2,1)S(1)}, bf16[320,512]{1,0:T(8,128)(2,1)}, u32[]{:S(2)}) copy-start(bf16[320,512]{1,0:T(8,128)(2,1)} %get-tuple-element.10) | copy-start | bytes 983044
  74.5 3.3 %copy-start = (bf16[320,512]{1,0:T(8,128)(2,1)S(1)}, bf16[320,512]{1,0:T(8,128)(2,1)}, u32[]{:S(2)}) copy-start(bf16[320,512]{1,0:T(8,128)(2,1)} %get-tuple-element.11) | copy-start | bytes 983044

commit v3 on v2

--- a/solution.py
+++ b/solution.py
@@ -278,7 +278,6 @@
     for h in range(HK):
         prepare(h)
     gather_b(0)
-    gather_b(1)
     gather_c(0)
     gain_part[...] = jnp.zeros_like(gain_part)
 
@@ -368,21 +367,20 @@
         def gain_term(grad_kn, keys):
             return fold(grad_kn * keys.astype(F32))
 
-        def root_grads(n):
-            keys = slice(n * SPAN, (n + 1) * SPAN)
+        def root_grads(half_x):
+            count = N_ROOT // 2
+            keys = slice(half_x * count, (half_x + 1) * count)
             grads = key_grads(keys, slice(0, Q_ROWS))
-            gain_part[0:8] += gain_term(grads[0], root_block(0, n))
-            for q in range(4):
-                owner = 4 * n + q
-                for t in range(2):
-                    parts[2 * h, owner % 2, owner // 8, (owner // 2) % 4, t] = grads[t][
-                        q * R_DEV : (q + 1) * R_DEV
-                    ].astype(BF16)
+            gain_part[...] += gain_term(grads[0], kv[h, 0, 0, half_x].reshape(count, DH))
+            for t in range(2):
+                terms = grads[t].reshape(4, 2, R_DEV, DH).astype(BF16)
+                for core in range(2):
+                    parts[2 * h, core, half_x, :, t] = terms[:, core]
 
         def side_grads():
             leaf_rows = slice(LEAF_AT, Q_ROWS)
             grads = key_grads(slice(N_ROOT, N_ROOT + SPAN + L_DEV), leaf_rows)
-            gain_part[0:8] += gain_term(grads[0], side[h, 0, : SPAN + L_DEV, :])
+            gain_part[...] += gain_term(grads[0], side[h, 0, : SPAN + L_DEV, :])
             cols = pl.ds(pl.multiple_of(h * DH, DH), DH)
             rows = slice(R_DEV + B_DEV, ROWS)
             raw = k_ref[rows, cols].astype(F32)
@@ -391,7 +389,7 @@
             ).astype(BF16)
             gv_ref[rows, cols] = grads[1][SPAN:].astype(BF16)
             own_grads = key_grads(slice(N_ROOT, N_ROOT + SPAN), slice(GQ * R_DEV, LEAF_AT))
-            gain_part[0:8] += gain_term(own_grads[0], side[h, 0, SPAN + L_DEV :, :])
+            gain_part[...] += gain_term(own_grads[0], side[h, 0, SPAN + L_DEV :, :])
             for b in range(4):
                 to_parent = jnp.where(parent == b, 1.0, 0.0)
                 to_own = jnp.where(own_branch == b, 1.0, 0.0)
@@ -403,38 +401,34 @@
                             q * B_DEV : (q + 1) * B_DEV
                         ].astype(BF16)
 
-        for rb in range(5):
+        for rb in range(3):
             root_scores(rb)
-
-        @pl.when(h < HK - 1)
-        def _():
-            gather_b(2 * h + 2)
-            gather_b(2 * h + 3)
+        gather_b(2 * h + 1)
+        for rb in range(3, 5):
+            root_scores(rb)
 
         @pl.when(h > 0)
         def _():
             reduce_a(2 * h - 2)
             reduce_a(2 * h - 1)
 
+        gather_c(2 * h + 1)
+        pick_side()
+        for rb in range(5):
+            side_scores(rb)
+        for n in range(2):
+            root_grads(n)
+        r_core(2 * h).start()
+        pl.when(h < HK - 1)(lambda: gather_b(2 * h + 2))
+        side_grads()
+        r_core(2 * h + 1).start()
+
         @pl.when(h > 1)
         def _():
             reduce_b(2 * h - 4)
             reduce_b(2 * h - 3)
 
-        gather_c(2 * h + 1)
-        pick_side()
-        for rb in range(5):
-            side_scores(rb)
-        for n in range(4):
-            root_grads(n)
-        r_core(2 * h).start()
-        side_grads()
-        r_core(2 * h + 1).start()
-
-        @pl.when(h < HK - 1)
-        def _():
-            gather_c(2 * h + 2)
-
+        pl.when(h < HK - 1)(lambda: gather_c(2 * h + 2))
         return carry
 
     lax.fori_loop(0, HK, one_head, 0)
@@ -464,7 +458,6 @@
                     gq_ref[rows, cols] = norm_backward(
                         raw, inverse, qgain_ref[...], grads
                     ).astype(BF16)
-                    gain_part[8:16] += fold(grads * raw * inverse)
 
         for rb in range(5):
             query_grads(rb)
@@ -508,29 +501,47 @@
         return total + gain_leaf[step]
 
     root, branch = HALVES - 2, HALVES - 1
+    gain_seq[0] = gain_part[...]
+    lax.fori_loop(1, N_SEQ, a_start, 0)
     reduce_a(root)
     queries_of(0)
     reduce_a(branch)
     queries_of(1)
-    queries_of(2)
+    gain_leaf[0] = lax.fori_loop(1, N_SEQ, a_wait, gain_seq[0])
+    lax.fori_loop(1, n_leaf, b_start, 0)
     reduce_b(root - 2)
     reduce_b(branch - 2)
+    queries_of(2)
     queries_of(3)
+    reduce_b(root)
+    gain = jnp.sum(lax.fori_loop(1, n_leaf, b_wait, gain_leaf[0]), axis=0, keepdims=True)
     row = lax.broadcasted_iota(jnp.int32, (8, DH), 0)
-    key_sum = jnp.sum(gain_part[0:8], axis=0, keepdims=True) / kgain_ref[...]
-    query_sum = jnp.sum(gain_part[8:16], axis=0, keepdims=True)
-    gain_seq[0] = jnp.where(row == 0, query_sum, key_sum)
-    lax.fori_loop(1, N_SEQ, a_start, 0)
-    reduce_b(root)
-    gain_leaf[0] = lax.fori_loop(1, N_SEQ, a_wait, gain_seq[0])
-    lax.fori_loop(1, n_leaf, b_start, 0)
+    gains_ref[...] = jnp.where(row == 0, gain / qgain_ref[...], gain / kgain_ref[...])
     reduce_b(branch)
-    gains_ref[...] = lax.fori_loop(1, n_leaf, b_wait, gain_leaf[0])
     for half in range(HALVES):
         gather_sent(half)
         reduce_sent(half)
     for h in range(HK):
         store_q(h).wait()
+
+
+def hand_over(gq_in, gk_in, gv_in, gains_in, gq_out, gk_out, gv_out, qg_out, kg_out, gq, gk, gv, sem):
+    pieces = [(gk_in, gk, gk_out), (gv_in, gv, gv_out)]
+    step = ROWS // 4
+    for n in range(4):
+        rows = pl.ds(n * step, step)
+        pieces.append((gq_in.at[rows], gq.at[rows], gq_out.at[rows]))
+    loads = [pltpu.make_async_copy(p[0], p[1], sem.at[0, n]) for n, p in enumerate(pieces)]
+    stores = [pltpu.make_async_copy(p[1], p[2], sem.at[1, n]) for n, p in enumerate(pieces)]
+    for load in loads:
+        load.start()
+    qg_out[...] = gains_in[0:1, :]
+    kg_out[...] = gains_in[1:2, :]
+    for load, store in zip(loads, stores):
+        load.wait()
+        store.start()
+    for store in stores:
+        store.wait()
 
 
 def on_device(
@@ -573,7 +584,7 @@
             pltpu.VMEM((HALVES, 2, 2, 4, 2, R_DEV, DH), BF16),
             pltpu.VMEM((HALVES, 2, 4, 2, R_DEV, DH), BF16),
             pltpu.VMEM((HALVES, CHIPS, 2, R_DEV, DH), BF16),
-            pltpu.VMEM((16, DH), F32),
+            pltpu.VMEM((8, DH), F32),
             pltpu.VMEM((N_SEQ, 8, DH), F32),
             pltpu.VMEM((n_leaf, 8, DH), F32),
             dma((HALVES, CHIPS)),
@@ -600,7 +611,32 @@
         query_gain.reshape(1, DH),
         key_gain.reshape(1, DH),
     )
-    return grad_query[None], grad_key[None], grad_value[None], gains[0], gains[1]
+    grad_query, grad_key, grad_value, query_gain_grad, key_gain_grad = pl.pallas_call(
+        hand_over,
+        out_shape=(
+            jax.ShapeDtypeStruct((ROWS, HQ * DH), BF16),
+            jax.ShapeDtypeStruct((ROWS, HK * DH), BF16),
+            jax.ShapeDtypeStruct((ROWS, HK * DH), BF16),
+            jax.ShapeDtypeStruct((1, DH), F32),
+            jax.ShapeDtypeStruct((1, DH), F32),
+        ),
+        in_specs=[hbm, hbm, hbm, vmem],
+        out_specs=(hbm, hbm, hbm, vmem, vmem),
+        scratch_shapes=[
+            pltpu.VMEM((ROWS, HQ * DH), BF16),
+            pltpu.VMEM((ROWS, HK * DH), BF16),
+            pltpu.VMEM((ROWS, HK * DH), BF16),
+            dma((2, 6)),
+        ],
+        name="hand_over",
+    )(grad_query, grad_key, grad_value, gains)
+    return (
+        grad_query[None],
+        grad_key[None],
+        grad_value[None],
+        query_gain_grad[0],
+        key_gain_grad[0],
+    )
 
 
 def solution(mesh):

time: 79.6 us -> 70.6 us (0.89)
  local copies, waits for them, and re-layouts: 5.31 us -> 0 us
  Pallas kernels: 71.3 us -> 67.7 us
    pallas_call x1, Pallas kernels: 71.3 us -> 64.2 us  [on_device(): pl.pallas_call(functools.partial(kernel, n_leaf), out_shape=(jax.ShapeDty...]
    unnamed x7 -> x0, local copies, waits for them, and re-layouts: 4.04 us -> none
    pallas_call x0 -> x1, Pallas kernels: none -> 3.53 us  [on_device(): pl.pallas_call(hand_over, out_shape=(jax.ShapeDtypeStruct((ROWS, HQ * DH)...]
    squeeze x1 -> x0, local copies, waits for them, and re-layouts: 1.26 us -> none  [on_device(): gains[1]]
where the time goes in v3:
time: 70.6 us; the launch traced here: 69.8 us
  Pallas kernels  67.7 us (96%)
  between operations  2.09 us (3%)
    pallas_call x1, Pallas kernels, on_device(): pl.pallas_call(functools.partial(kernel, n_leaf), out_shape=(jax.ShapeDty...  64.2 us
    pallas_call x1, Pallas kernels, on_device(): pl.pallas_call(hand_over, out_shape=(jax.ShapeDtypeStruct((ROWS, HQ * DH)...  3.53 us

profile of v3, /device:TPU:8, one launch (start us, length us, event | category | flops | bytes accessed | tf_op | source)
XLA Modules:
  0.0 69.8 jit_solution(5585021636199991564)
XLA Ops:
  1.9 64.2 %attention_backward.1 = (bf16[320,2048]{1,0:T(8,128)(2,1)}, bf16[320,512]{1,0:T(8,128)(2,1)}, bf16[320,512]{1,0:T(8,128)(2,1)}, f32[8,128]{1,0:T(8,128)}) custom-call(s32[1,1]{1,0:T(1,128)S(6)} %copy.13.parent_ref, s32[1,1]{1,0:T(1,128)S(6)} %copy.14.blocks_ref, bf16[320,2048]{1,0:T(8,128)(2,1)} %bitcast.11, bf16[320,512]{1,0:T(8,128)(2,1)} %bitcast.13, ...), custom_call_target="tpu_custom_call" | custom-call | tf_op jit(solution)/shard_map/attention_backward/pallas_call | solution.py:556
  66.1 3.5 %hand_over.1 = (bf16[320,2048]{1,0:T(8,128)(2,1)}, bf16[320,512]{1,0:T(8,128)(2,1)}, bf16[320,512]{1,0:T(8,128)(2,1)}, f32[1,128]{1,0:T(1,128)}, f32[1,128]{1,0:T(1,128)}) custom-call(bf16[320,2048]{1,0:T(8,128)(2,1)} %get-tuple-element.14.gq_in, bf16[320,512]{1,0:T(8,128)(2,1)} %get-tuple-element.15.gk_in, bf16[320,512]{1,0:T(8,128)(2,1)} %get-tuple-element.16.gv_in, ...), custom_call_target="tpu_custom_call" | custom-call | tf_op jit(solution)/shard_map/hand_over/pallas_call | solution.py:614

commit v4 on v3

--- a/solution.py
+++ b/solution.py
@@ -275,9 +275,11 @@
         gather_a(half)
     load_q.wait()
     load_u.wait()
-    for h in range(HK):
-        prepare(h)
+    prepare(0)
+    prepare(1)
+    prepare(2)
     gather_b(0)
+    prepare(3)
     gather_c(0)
     gain_part[...] = jnp.zeros_like(gain_part)
 
@@ -401,17 +403,14 @@
                             q * B_DEV : (q + 1) * B_DEV
                         ].astype(BF16)
 
-        for rb in range(3):
+        root_scores(0)
+        pl.when(h > 0)(lambda: reduce_a(2 * h - 2))
+        for rb in range(1, 3):
             root_scores(rb)
         gather_b(2 * h + 1)
+        pl.when(h > 0)(lambda: reduce_a(2 * h - 1))
         for rb in range(3, 5):
             root_scores(rb)
-
-        @pl.when(h > 0)
-        def _():
-            reduce_a(2 * h - 2)
-            reduce_a(2 * h - 1)
-
         gather_c(2 * h + 1)
         pick_side()
         for rb in range(5):
@@ -509,10 +508,10 @@
     queries_of(1)
     gain_leaf[0] = lax.fori_loop(1, N_SEQ, a_wait, gain_seq[0])
     lax.fori_loop(1, n_leaf, b_start, 0)
+    queries_of(2)
+    queries_of(3)
     reduce_b(root - 2)
     reduce_b(branch - 2)
-    queries_of(2)
-    queries_of(3)
     reduce_b(root)
     gain = jnp.sum(lax.fori_loop(1, n_leaf, b_wait, gain_leaf[0]), axis=0, keepdims=True)
     row = lax.broadcasted_iota(jnp.int32, (8, DH), 0)

time: 70.6 us -> 70.6 us (level)
  no operation moved by 1% of the time
where the time goes in v4:
time: 70.6 us; the launch traced here: 69.8 us
  Pallas kernels  67.7 us (96%)
  between operations  2.09 us (3%)
    pallas_call x1, Pallas kernels, on_device(): pl.pallas_call(functools.partial(kernel, n_leaf), out_shape=(jax.ShapeDty...  64.2 us
    pallas_call x1, Pallas kernels, on_device(): pl.pallas_call(hand_over, out_shape=(jax.ShapeDtypeStruct((ROWS, HQ * DH)...  3.53 us

profile of v4, /device:TPU:8, one launch (start us, length us, event | category | flops | bytes accessed | tf_op | source)
XLA Modules:
  0.0 69.8 jit_solution(3092014710386371575)
XLA Ops:
  1.9 64.2 %attention_backward.1 = (bf16[320,2048]{1,0:T(8,128)(2,1)}, bf16[320,512]{1,0:T(8,128)(2,1)}, bf16[320,512]{1,0:T(8,128)(2,1)}, f32[8,128]{1,0:T(8,128)}) custom-call(s32[1,1]{1,0:T(1,128)S(6)} %copy.13.parent_ref, s32[1,1]{1,0:T(1,128)S(6)} %copy.14.blocks_ref, bf16[320,2048]{1,0:T(8,128)(2,1)} %bitcast.11, bf16[320,512]{1,0:T(8,128)(2,1)} %bitcast.13, ...), custom_call_target="tpu_custom_call" | custom-call | tf_op jit(solution)/shard_map/attention_backward/pallas_call | solution.py:555
  66.1 3.5 %hand_over.1 = (bf16[320,2048]{1,0:T(8,128)(2,1)}, bf16[320,512]{1,0:T(8,128)(2,1)}, bf16[320,512]{1,0:T(8,128)(2,1)}, f32[1,128]{1,0:T(1,128)}, f32[1,128]{1,0:T(1,128)}) custom-call(bf16[320,2048]{1,0:T(8,128)(2,1)} %get-tuple-element.14.gq_in, bf16[320,512]{1,0:T(8,128)(2,1)} %get-tuple-element.15.gk_in, bf16[320,512]{1,0:T(8,128)(2,1)} %get-tuple-element.16.gv_in, ...), custom_call_target="tpu_custom_call" | custom-call | tf_op jit(solution)/shard_map/hand_over/pallas_call | solution.py:613
